TPU v7x, 256 devices: a whole 4x4x8 slice. The times are simulated.
256 devices in a mesh: fsdp: 32 (over z, x_lo, core), tenant: 4 (over y), tensor: 2 (over x_hi).
Axes of the slice: x: 4 (x_hi: 2, x_lo: 2; x = x_hi * 2 + x_lo), y: 4, z: 8, core: 2. Of those that a mesh axis runs over, the one named last changes fastest.
Arguments:
- tokens: bfloat16 [16384, 8192], P(('fsdp', 'tenant')), may hold values from -6 to 6
- inner_x: bfloat16 [16384, 8192], P(('fsdp', 'tenant'), 'tensor'), may hold values from -6 to 6
- step_size: float32 [16384, 128], P(('fsdp', 'tenant'), 'tensor'), may hold values from 0.01 to 0.25
- decay_rate: float32 [128], P('tensor'), may hold values from 0.2 to 16
- grad_out: bfloat16 [16384, 8192], P(('fsdp', 'tenant'), 'tensor'), may hold values from -6 to 6
- w_bc: bfloat16 [8192, 2048], P('fsdp', 'tensor'), may hold values from -0.0625 to 0.0625
- a_store: bfloat16 [256, 8192, 64], P(('fsdp', 'tenant'), 'tensor'), may hold values from -0.0625 to 0.0625
- b_store: bfloat16 [256, 64, 2048], P(('fsdp', 'tenant'), None, 'tensor'), may hold values from -0.75 to 0.75
- tenant_list: int32 [4, 2], P('tenant'), may hold values from 0 to 255, as said below
- block_slot: int32 [128], P(('fsdp', 'tenant')), may hold values from 0 to 1, as said below
- owner_slot: int32 [256], replicated, may hold values from 0 to 255, as said below
Outputs:
- mixed_out: bfloat16 [16384, 8192], P(('fsdp', 'tenant'), 'tensor')
- input_grad: bfloat16 [16384, 8192], P(('fsdp', 'tenant'), 'tensor')
- a_grad: bfloat16 [256, 8192, 64], P(('fsdp', 'tenant'), 'tensor')
- b_grad: bfloat16 [256, 64, 2048], P(('fsdp', 'tenant'), None, 'tensor')
Inputs may be any that keep to these rules, and one draw needn't show every extreme that they name: `tenant_list`: row g lists the tenants of data group g; entries of a row are distinct. `block_slot`: sample b belongs to data group (b) mod 4. In each group the positions used are 0 up to some count, each used by some sample; the count is 2 in some group. Tenant t's adapters are row owner_slot[t] of a_store and b_store; every row belongs to exactly one tenant. The row owner_slot[tenant_list[g, j]] lies on the devices of tenant index (g + 2 - j) mod 4.
All inputs are finite; a program needn't handle non-finite values.
Results may differ from a plain program's by a relative error of at most 0.012.
Values may be sent and summed in bfloat16 or wider, within the bound.
A program may use at most 320 MiB of HBM per device.

v0:
```python
import jax
import jax.numpy as jnp
from jax import lax
from jax.sharding import PartitionSpec as P

HEADS_GRP = 32
NS = 256


def spread_2(block, axis, holder):
    block = jnp.where(lax.axis_index(axis) == holder, block, jnp.zeros_like(block))
    return lax.psum(block, axis)


def mix_state(proj_in, inner_x, step_size, decay_rate, block_len, heads_grp, state_dim):
    length = proj_in.shape[0]
    nblock = length // block_len
    groups = proj_in.shape[1] // (2 * state_dim)
    num_heads = decay_rate.shape[0]
    head_dim = inner_x.shape[1] // num_heads
    split_proj = proj_in.reshape(nblock, block_len, groups, 2, state_dim)
    b_input = split_proj[:, :, :, 0, :]
    c_output = split_proj[:, :, :, 1, :]
    values = inner_x.astype(jnp.float32).reshape(nblock, block_len, groups, heads_grp, head_dim)
    step_blk = step_size.reshape(nblock, block_len, groups, heads_grp)
    log_decay = -step_blk * decay_rate.reshape(groups, heads_grp)
    totals = jnp.cumsum(log_decay, axis=1)
    spread = totals[:, :, None] - totals[:, None, :]
    causal = jnp.arange(block_len)[:, None] >= jnp.arange(block_len)[None, :]
    decay_mat = jnp.exp(jnp.where(causal[None, :, :, None, None], spread, -1e30))
    scores = jnp.einsum("ntgk,nsgk->ntsg", c_output, b_input, precision=lax.Precision.HIGHEST)
    weight = decay_mat * scores[..., None] * step_blk[:, None]
    mixed_all = jnp.einsum("ntsgh,nsghp->ntghp", weight, values, precision=lax.Precision.HIGHEST)
    return mixed_all.reshape(length, num_heads * head_dim)


def shards(
    tokens,
    inner_x,
    step_size,
    decay_rate,
    grad_out,
    w_bc,
    a_store,
    b_store,
    tenant_list,
    block_slot,
    owner_slot,
):
    tenant_span = lax.axis_size("tenant")
    fsdp_here = lax.axis_index("fsdp")
    tensor_here = lax.axis_index("tensor")
    owned = a_store.shape[0]
    width_half = a_store.shape[1]
    length = tokens.shape[0]
    nblock = block_slot.shape[0]
    block_len = length // nblock
    list_len = tenant_list.shape[1]
    columns = w_bc.shape[1]
    my_list = tenant_list[0]
    location = owner_slot[my_list]
    holder = location // owned
    root_fsdp = holder // tenant_span
    pool_index = holder % tenant_span * owned + location % owned
    pool_a, pool_b = (
        lax.all_gather(a_store, "tenant", axis=0, tiled=True),
        lax.all_gather(b_store, "tenant", axis=0, tiled=True),
    )
    fetched_a = []
    fetched_b = []
    for position in range(list_len):
        got_a, got_b = (
            spread_2(pool_a[pool_index[position]], "fsdp", root_fsdp[position]),
            spread_2(pool_b[pool_index[position]], "fsdp", root_fsdp[position]),
        )
        fetched_a.append(got_a)
        fetched_b.append(got_b)
    list_a = jnp.stack(fetched_a)
    list_b = jnp.stack(fetched_b)
    token_half = lax.dynamic_slice_in_dim(tokens, tensor_here * width_half, width_half, 1)
    sel_a = list_a[block_slot]
    sel_b = list_b[block_slot]
    half_blocks = token_half.reshape(nblock, block_len, width_half)
    part_low = jnp.einsum("nbd,ndr->nbr", half_blocks, sel_a, preferred_element_type=jnp.float32)
    low_rank = lax.psum(part_low, "tensor").astype(jnp.bfloat16)
    whole_w = lax.all_gather(w_bc, "fsdp", axis=0, tiled=True)
    base_proj = jnp.dot(tokens, whole_w, preferred_element_type=jnp.float32)
    adapter_proj = jnp.einsum("nbr,nrc->nbc", low_rank, sel_b, preferred_element_type=jnp.float32)
    proj = (base_proj + adapter_proj.reshape(length, columns)).astype(jnp.bfloat16)

    def mixer(proj_in):
        return mix_state(proj_in, inner_x, step_size, decay_rate, block_len, HEADS_GRP, NS)

    mixed_now, pull_back = jax.vjp(mixer, proj.astype(jnp.float32))
    (grad_proj,) = pull_back(grad_out.astype(jnp.float32))
    grad_proj = grad_proj.astype(jnp.bfloat16)
    grad_blocks = grad_proj.reshape(nblock, block_len, columns)
    part_q = jnp.einsum("nbc,nrc->nbr", grad_blocks, sel_b, preferred_element_type=jnp.float32)
    q_low = lax.psum(part_q, "tensor").astype(jnp.bfloat16)
    part_input = jnp.dot(grad_proj, whole_w.T, preferred_element_type=jnp.float32)
    summed_input = lax.psum_scatter(part_input, "tensor", scatter_dimension=1, tiled=True)
    adapter_input = jnp.einsum("nbr,ndr->nbd", q_low, sel_a, preferred_element_type=jnp.float32)
    input_grad = (summed_input + adapter_input.reshape(length, width_half)).astype(jnp.bfloat16)
    grad_a_blk = jnp.einsum("nbd,nbr->ndr", half_blocks, q_low, preferred_element_type=jnp.float32)
    grad_b_blk = jnp.einsum(
        "nbr,nbc->ncr", low_rank, grad_blocks, preferred_element_type=jnp.float32
    )
    chosen = (block_slot[:, None] == jnp.arange(list_len)[None, :]).astype(jnp.float32)
    list_grad_a = jnp.einsum("nl,ndr->ldr", chosen, grad_a_blk, precision=lax.Precision.HIGHEST)
    list_grad_b = jnp.einsum("nl,ncr->lcr", chosen, grad_b_blk, precision=lax.Precision.HIGHEST)
    group_a, group_b = lax.psum((list_grad_a, list_grad_b), "fsdp")
    round_a = group_a.astype(jnp.bfloat16)
    round_b = group_b.astype(jnp.bfloat16)
    round_b = jnp.swapaxes(round_b, 1, 2)
    send_hot = (
        (pool_index[:, None] == jnp.arange(tenant_span * owned)[None, :])
        & (root_fsdp == fsdp_here)[:, None]
    ).astype(jnp.bfloat16)
    send_a = jnp.einsum("lk,ldr->kdr", send_hot, round_a, preferred_element_type=jnp.float32)
    send_b = jnp.einsum("lk,lrc->krc", send_hot, round_b, preferred_element_type=jnp.float32)
    owner_a, owner_b = (
        lax.psum_scatter(
            send_a.astype(jnp.bfloat16), "tenant", scatter_dimension=0, tiled=True
        ).astype(jnp.float32),
        lax.psum_scatter(
            send_b.astype(jnp.bfloat16), "tenant", scatter_dimension=0, tiled=True
        ).astype(jnp.float32),
    )
    return (
        mixed_now.astype(jnp.bfloat16),
        input_grad,
        owner_a.astype(jnp.bfloat16),
        owner_b.astype(jnp.bfloat16),
    )


def solution(mesh):
    placed = (
        P(("fsdp", "tenant"), None),
        P(("fsdp", "tenant"), "tensor"),
        P(("fsdp", "tenant"), "tensor"),
        P("tensor"),
        P(("fsdp", "tenant"), "tensor"),
        P("fsdp", "tensor"),
        P(("fsdp", "tenant"), "tensor", None),
        P(("fsdp", "tenant"), None, "tensor"),
        P("tenant", None),
        P(("fsdp", "tenant")),
        P(),
    )
    return jax.shard_map(
        shards,
        mesh=mesh,
        in_specs=placed,
        out_specs=(
            P(("fsdp", "tenant"), "tensor"),
            P(("fsdp", "tenant"), "tensor"),
            P(("fsdp", "tenant"), "tensor", None),
            P(("fsdp", "tenant"), None, "tensor"),
        ),
        check_vma=False,
    )
```

profile of v0, /device:TPU:1, one launch (start us, length us, event | category | flops | bytes accessed | tf_op | source)
XLA Modules:
  0.0 697.1 jit_solution(18225526234914856644)
XLA Ops:
  7.3 0.7 all-gather.8.cloned.1.call-update
  8.0 0.7 all-gather.6.cloned.1.call-update
  8.7 0.7 fusion.52
  9.4 1.3 gather_fusion
  14.5 0.6 fusion.61
  17.7 21.7 %all-gather.8.cloned.1.call-done = bf16[8,64,1024]{2,1,0:T(8,128)(2,1)} async-done(((bf16[2,64,1024]{2,1,0:T(8,128)(2,1)}), bf16[8,64,1024]{2,1,0:T(8,128)(2,1)}) %all-gather.8.cloned.1.call-update) | async-done | bytes 1048592 | tf_op jit(solution)/shard_map/all_gather | solution.py:67
  39.3 1.7 dynamic-slice_select_fusion.2
  41.0 52.2 %all-gather.6.cloned.1.call-done = bf16[8,4096,64]{1,2,0:T(8,128)(2,1)} async-done(((bf16[2,4096,64]{1,2,0:T(8,128)(2,1)}), bf16[8,4096,64]{1,2,0:T(8,128)(2,1)}) %all-gather.6.cloned.1.call-update) | async-done | bytes 4194320 | tf_op jit(solution)/shard_map/all_gather | solution.py:66
  93.3 2.2 dynamic-slice_select_fusion
  97.2 1.3 copy.51
  98.5 1.6 copy.54
  100.2 3.6 fusion.2
  103.8 222.9 %all-reduce.7.cloned.1.call-done = (bf16[1,4096,64]{1,2,0:T(8,128)(2,1)}, bf16[1,4096,64]{1,2,0:T(8,128)(2,1)}, bf16[1,64,1024]{2,1,0:T(8,128)(2,1)}, bf16[1,64,1024]{2,1,0:T(8,128)(2,1)}) async-done(((bf16[1,4096,64]{1,2,0:T(8,128)(2,1)}, bf16[1,4096,64]{1,2,0:T(8,128)(2,1)}, bf16[1,64,1024]{2,1,0:T(8,128)(2,1)}, bf16[1,64,1024]{2,1,0:T(8,128)(2,1)}), (bf16[1,4096,64]{1,2,0:T(8,128)(2,1)}, ...) | async-done | bytes 1310736 | tf_op jit(solution)/shard_map/psum | solution.py:12
  326.7 1.5 convolution_bitcast_fusion.3
  328.2 8.9 %psum.58 = bf16[1,128,64]{1,2,0:T(8,128)(2,1)S(1)} all-reduce(f32[1,128,64]{1,2,0:T(8,128)S(1)} %convolution_bitcast_fusion.3), channel_id=1, replica_groups=mesh['fsdp'=32,'tenant'=4,'tensor'=2] {'tensor'}, use_global_device_ids=true, to_apply=%region_3.4 | all-reduce | flops 8192 | bytes 49152 | tf_op jit(solution)/shard_map/psum | solution.py:85
  337.2 91.7 %all-gather.4.cloned.1.call-done = bf16[8192,1024]{1,0:T(8,128)(2,1)} async-done(((bf16[256,1024]{1,0:T(8,128)(2,1)}), bf16[8192,1024]{1,0:T(8,128)(2,1)}) %all-gather.4.cloned.1.call-update) | async-done | bytes 16777232 | tf_op jit(solution)/shard_map/all_gather | solution.py:86
  428.8 8.1 %fusion.63 = f32[128,1024]{1,0:T(8,128)S(1)} fusion(bf16[128,8192]{1,0:T(8,128)(2,1)S(1)} %copy-done, bf16[8192,1024]{1,0:T(8,128)(2,1)} %all-gather.4.cloned.1.call-done), kind=kOutput, calls=%fused_computation.97 | convolution fusion | flops 2147483648 | bytes 19398656 | tf_op jit(solution)/shard_map/dot_general | solution.py:87
  439.0 13.5 %fusion.64 = f32[128,8192]{1,0:T(8,128)} fusion(bf16[128,1024]{0,1:T(8,128)(2,1)S(1)} %bitcast.109, bf16[8192,1024]{1,0:T(8,128)(2,1)} %all-gather.4.cloned.1.call-done), kind=kOutput, calls=%fused_computation.98 | convolution fusion | flops 2147483648 | bytes 21233664 | tf_op jit(solution)/shard_map/dot_general | solution.py:100
  453.0 1.1 convolution_bitcast_fusion.4
  454.1 9.6 %psum.61 = bf16[1,128,64]{1,2,0:T(8,128)(2,1)S(1)} all-reduce(f32[1,128,64]{1,2,0:T(8,128)S(1)} %convolution_bitcast_fusion.4), channel_id=1, replica_groups=mesh['fsdp'=32,'tenant'=4,'tensor'=2] {'tensor'}, use_global_device_ids=true, to_apply=%region_8.9 | all-reduce | flops 8192 | bytes 49152 | tf_op jit(solution)/shard_map/psum | solution.py:99
  464.1 3.2 broadcast_multiply_fusion
  467.3 137.2 %all-reduce.8 = (bf16[2,4096,64]{1,0,2:T(2,128)(2,1)}, bf16[2,1024,64]{1,0,2:T(2,128)(2,1)}) all-reduce(f32[2,4096,64]{1,0,2:T(2,128)} %broadcast_multiply_fusion, f32[2,1024,64]{1,0,2:T(2,128)S(1)} %broadcast_multiply_fusion.1), channel_id=1, replica_groups=mesh['fsdp'=32,'tenant'=4,'tensor'=2] {'fsdp'}, use_global_device_ids=true, to_apply=%region_9.10 | all-reduce | flops 655360 | bytes 3932160 | tf_op jit(solution)/shard_map/psum | solution.py:111
  604.5 1.6 convolution_convert_fusion.1
  606.1 1.6 copy.58
  607.8 1.9 convolution_convert_fusion
  609.7 4.2 copy.57
  613.9 1.2 convolution_bitcast_fusion.2
  615.3 7.0 %fusion.15 = bf16[2,32,128,64]{2,3,1,0:T(8,128)(2,1)} fusion(bf16[128,2,32,64]{0,3,2,1:T(8,128)(2,1)S(1)} %bitcast.113, f32[128,2,32]{0,2,1:T(8,128)} %bitcast.116, f32[128,128,2]{1,0,2:T(8,128)S(1)} %copy.50, f32[128,2,32]{0,2,1:T(8,128)} %copy-done.9, pred[128,128]{1,0:T(8,128)(4,1)} %copy-done.10), kind=kOutput, calls=%fused_computation.19 | convolution fusion | flops 810024960 | bytes 2310144 | tf_op jit(solution)/shard_map/jvp(ntsgh,nsghp->ntghp)/dot_general | solution.py:33
  622.3 2.3 copy.59
  624.6 3.2 fusion
  627.8 8.1 %reduce-scatter.8.cloned.1.call-done = bf16[2,64,1024]{2,1,0:T(8,128)(2,1)} async-done(((bf16[8,64,1024]{2,1,0:T(8,128)(2,1)}), bf16[2,64,1024]{2,1,0:T(8,128)(2,1)}) %reduce-scatter.8.cloned.1.call-update) | async-done | bytes 262160 | tf_op jit(solution)/shard_map/reduce_scatter | solution.py:125
  636.0 54.3 %reduce-scatter.6.cloned.1.call-done = bf16[2,4096,64]{1,2,0:T(8,128)(2,1)} async-done(((bf16[8,4096,64]{1,2,0:T(8,128)(2,1)}), bf16[2,4096,64]{1,2,0:T(8,128)(2,1)}) %reduce-scatter.6.cloned.1.call-update) | async-done | bytes 1048592 | tf_op jit(solution)/shard_map/reduce_scatter | solution.py:122
  (66 shorter events, 5.3 us)
Async XLA Ops:
  7.2 319.5 %copy-start = (bf16[128,8192]{1,0:T(8,128)(2,1)S(1)}, bf16[128,8192]{1,0:T(8,128)(2,1)}, u32[]{:S(2)}) copy-start(bf16[128,8192]{1,0:T(8,128)(2,1)} %param.11) | copy-start | bytes 6291460
  7.2 89.6 %copy-start.15 = (f32[64]{0:T(128)S(1)}, f32[64]{0:T(128)}, u32[]{:S(2)}) copy-start(f32[64]{0:T(128)} %param.14) | copy-start | bytes 772
  7.2 89.7 %copy-start.8 = (f32[128,64]{0,1:T(8,128)S(1)}, f32[128,64]{0,1:T(8,128)}, u32[]{:S(2)}) copy-start(f32[128,64]{0,1:T(8,128)} %param.13) | copy-start | bytes 98308
  7.2 90.0 %copy-start.1 = (bf16[128,4096]{1,0:T(8,128)(2,1)S(1)}, bf16[128,4096]{1,0:T(8,128)(2,1)}, u32[]{:S(2)}) copy-start(bf16[128,4096]{1,0:T(8,128)(2,1)} %param.12) | copy-start | bytes 3145732
  7.2 32.1 %all-gather.8.cloned.1.call-start = ((), (), s32[]{:S(2)}) async-start(), calls=%async_computation.5 | async-start | bytes 1310720 | tf_op jit(solution)/shard_map/all_gather | solution.py:67
  7.9 85.3 %all-gather.6.cloned.1.call-start = ((), (), s32[]{:S(2)}) async-start(), calls=%async_computation.4 | async-start | bytes 5242880 | tf_op jit(solution)/shard_map/all_gather | solution.py:66
  8.7 318.0 %all-reduce.7.cloned.1.call-start = ((), (), s32[]{:S(2)}) async-start(), calls=%async_computation.9 | async-start | bytes 2621440 | tf_op jit(solution)/shard_map/psum | solution.py:12
  11.3 85.6 %copy-start.11 = (s32[2]{0:T(128)}, s32[2]{0:T(128)S(1)}, u32[]{:S(2)}) copy-start(s32[2]{0:T(128)S(1)} %fusion.50) | copy-start | bytes 28
  95.5 333.3 %all-gather.4.cloned.1.call-start = ((), (), s32[]{:S(2)}) async-start(), calls=%async_computation.3 | async-start | bytes 17301504 | tf_op jit(solution)/shard_map/all_gather | solution.py:86
  96.1 528.5 %reduce-scatter.4.cloned.1.call-start = ((), (), s32[]{:S(2)}) async-start(), calls=%async_computation.6 | async-start | bytes 6291456 | tf_op jit(solution)/shard_map/reduce_scatter | solution.py:101
  97.2 6.6 copy-start.9
  100.2 3.6 copy-start.10
  337.2 99.8 %copy-start.5 = (bf16[1,64,1024]{2,1,0:T(8,128)(2,1)S(1)}, bf16[1,64,1024]{2,1,0:T(8,128)(2,1)}, u32[]{:S(2)}) copy-start(bf16[1,64,1024]{2,1,0:T(8,128)(2,1)} %get-tuple-element.42) | copy-start | bytes 393220
  337.2 99.8 %copy-start.6 = (bf16[1,64,1024]{2,1,0:T(8,128)(2,1)S(1)}, bf16[1,64,1024]{2,1,0:T(8,128)(2,1)}, u32[]{:S(2)}) copy-start(bf16[1,64,1024]{2,1,0:T(8,128)(2,1)} %get-tuple-element.43) | copy-start | bytes 393220
  337.2 100.6 %copy-start.7 = (f32[128,128,2]{1,0,2:T(8,128)S(1)}, f32[128,128,2]{1,0,2:T(8,128)}, u32[]{:S(2)}) copy-start(f32[128,128,2]{1,0,2:T(8,128)} %fusion.2) | copy-start | bytes 393220
  437.8 0.7 copy-start.3
  452.4 183.5 %reduce-scatter.8.cloned.1.call-start = ((), (), s32[]{:S(2)}) async-start(), calls=%async_computation.8 | async-start | bytes 1310720 | tf_op jit(solution)/shard_map/reduce_scatter | solution.py:125
  452.5 0.5 copy-start.14
  454.1 150.4 %copy-start.12 = (s32[2]{0:T(128)S(1)}, s32[2]{0:T(128)}, u32[]{:S(2)}) copy-start(s32[2]{0:T(128)} %copy-done.11) | copy-start | bytes 28
  454.1 150.4 %copy-start.13 = (pred[2]{0:T(512)(128)(4,1)S(1)}, pred[2]{0:T(512)(128)(4,1)}, u32[]{:S(2)}) copy-start(pred[2]{0:T(512)(128)(4,1)} %get-tuple-element.44) | copy-start | bytes 10
  604.5 3.3 copy-start.4
  607.7 82.6 %reduce-scatter.6.cloned.1.call-start = ((), (), s32[]{:S(2)}) async-start(), calls=%async_computation.7 | async-start | bytes 5242880 | tf_op jit(solution)/shard_map/reduce_scatter | solution.py:122
  613.9 1.4 copy-start.2
Sparse Core Ops, SparseCore 0:
  9.9 29.4 all-gather.7
  41.1 52.0 all-gather.5
  96.7 229.9 all-reduce.6
  328.5 100.2 all-gather.3
  452.6 83.5 reduce-scatter.3
  607.8 28.0 reduce-scatter.7
  639.2 51.0 reduce-scatter.5
where the time goes:
time: 698 us; the launch traced here: 697 us
  waiting for transfers between devices  453 us (65%)
  blocking collectives  156 us (22%)
  matrix products  44 us (6%)
  between operations  20.3 us (3%)
  local copies, waits for them, and re-layouts  15.1 us (2%)
  other arithmetic  8.8 us (1%)
    psum x1, waiting for transfers between devices, spread_2(): return lax.psum(block, axis)  223 us
    psum x1, blocking collectives, shards(): group_a, group_b = lax.psum((list_grad_a, list_grad_b), 'fsdp')  137 us
    all_gather x1, waiting for transfers between devices, shards(): whole_w = lax.all_gather(w_bc, 'fsdp', axis=0, tiled=True)  91.7 us
    reduce_scatter x1, waiting for transfers between devices, shards(): lax.psum_scatter(send_a.astype(jnp.bfloat16), 'tenant', scatter_dimension...  54.3 us
    all_gather x1, waiting for transfers between devices, shards(): lax.all_gather(a_store, 'tenant', axis=0, tiled=True)  52.2 us
    all_gather x1, waiting for transfers between devices, shards(): lax.all_gather(b_store, 'tenant', axis=0, tiled=True)  21.7 us
  transfers between devices with their start and end apart: 7, of which 6 were waited for; matrix products, arithmetic and copies ran while one was open for 6% of the time, Pallas kernels for 0%

commit v1 on v0

v1 whole, which is shorter than its diff:
```python
import jax
import jax.numpy as jnp
from jax import lax
from jax.experimental import pallas as pl
from jax.experimental.pallas import tpu as pltpu
from jax.sharding import PartitionSpec as P

MESH = pl.DeviceIdType.MESH
F32 = jnp.float32
BF16 = jnp.bfloat16
NZ = 8
HEADS_GRP = 32
NS = 256

X_, Z_, Y_, D_ = 0, 2, 18, 34
LIST_, FCORE, FX, FZ_, FY, GZ_, GX, GCORE, LOW = 50, 52, 53, 54, 62, 63, 71, 72, 73
Q, PIN_, BCORE, BZ_, BX, BY, HX, HZ_, HCORE = 74, 75, 79, 80, 88, 89, 90, 91, 99
SLOTS = 100

NN = (((1,), (0,)), ((), ()))
NT = (((1,), (1,)), ((), ()))
TN = (((0,), (0,)), ((), ()))


def dot(a, b, dims=NN, precision=None):
    return lax.dot_general(a, b, dims, precision=precision, preferred_element_type=F32)


def body(
    slot_ref, tok_hbm, x_hbm, step_ref, rate_ref, g_hbm, w_hbm, a_hbm, b_hbm, loc_ref,
    mixed_hbm, igrad_hbm, agrad_hbm, bgrad_hbm,
    w, tok, x, g, a_own, b_own, listed, cand, rcore, rx, rz, chunk, ry, full,
    sel_a, sel_b, low_s, low_r, low_t, decay, tot, score_grad, acc, proj, gproj,
    q_s, q_r, q_t, psend, precv, part, mixed, igrad,
    bcand, brcore, brz, bs, brx, bchunk, bry, bfull, agrad, bgrad,
    ssem, rsem, lsem,
):
    f = lax.axis_index("fsdp")
    y = lax.axis_index("tenant")
    t = lax.axis_index("tensor")
    z = f // 4
    l = (f // 2) % 2
    c = f % 2
    p = y % 2
    rows = tok.shape[0]
    pairs = x.shape[1] // 128
    grp_pairs = pairs // 2

    def zat(d):
        return (z + d + NZ) % NZ

    def zdev(d):
        return (zat(d) * 4 + l * 2 + c, y, t)

    def ydev(d):
        return (f, (y + d + 4) % 4, t)

    sib = (z * 4 + l * 2 + (1 - c), y, t)
    xdev = (z * 4 + (1 - l) * 2 + c, y, t)
    tdev = (f, y, 1 - t)

    sent = []

    def send(src, dst, slot, dev):
        copy = pltpu.make_async_remote_copy(
            src_ref=src, dst_ref=dst, send_sem=ssem.at[slot], recv_sem=rsem.at[slot],
            device_id=dev, device_id_type=MESH,
        )
        copy.start()
        sent.append(copy)

    def got(dst, slot):
        pltpu.make_async_remote_copy(
            src_ref=dst, dst_ref=dst, send_sem=ssem.at[slot], recv_sem=rsem.at[slot],
            device_id=sib, device_id_type=MESH,
        ).wait_recv()

    def local(src, dst, slot):
        copy = pltpu.make_async_copy(src, dst, lsem.at[slot])
        copy.start()
        return copy

    def lside(which):
        return l if which == 0 else 1 - l

    def piece(d, which, par):
        first = pl.multiple_of((lside(which) * 2 + c) * 256 + par * 128, 128)
        return w.at[zat(d), pl.ds(first, 128), :]

    def whole(d, which, core):
        first = pl.multiple_of((lside(which) * 2 + core) * 256, 256)
        return w.at[zat(d), pl.ds(first, 256), :]

    load_w = local(w_hbm, whole(0, 0, c), 0)
    load_a = local(a_hbm, a_own, 1)
    load_b = local(b_hbm, b_own, 2)
    load_x = local(x_hbm, x, 3)
    load_g = local(g_hbm, g, 4)
    load_tok = local(tok_hbm, tok, 5)

    barrier = pltpu.get_barrier_semaphore()
    partners = [sib, xdev, tdev] + [zdev(d) for d in range(1, NZ)] + [ydev(d) for d in range(1, 4)]
    for dev in partners:
        pl.semaphore_signal(barrier, inc=1, device_id=dev, device_id_type=MESH)
    pl.semaphore_wait(barrier, len(partners))

    for j in range(2):
        send(loc_ref, listed.at[j], LIST_ + j, ydev(2 - j))
    load_w.wait()
    send(piece(0, 0, p), piece(0, 0, p), X_, xdev)
    for way in range(2):
        send(piece(0, 0, p), piece(0, 0, p), Z_ + way * 8, zdev(1 - 2 * way))
    send(piece(0, 0, 1 - p), piece(0, 0, 1 - p), X_ + 1, xdev)
    send(whole(0, 0, c), whole(0, 0, c), D_, sib)

    upto = (
        lax.broadcasted_iota(jnp.int32, (rows, rows), 0)
        <= lax.broadcasted_iota(jnp.int32, (rows, rows), 1)
    ).astype(F32)
    tot[...] = dot(-step_ref[...] * rate_ref[...], upto, precision=lax.Precision.HIGHEST)
    score_grad[...] = jnp.zeros_like(score_grad)
    load_x.wait()
    load_g.wait()

    lanes = lax.broadcasted_iota(jnp.int32, (rows, 128), 1)

    def split_heads(values):
        wide = values.astype(F32)
        one = jnp.where(lanes < 64, wide, 0.0).astype(BF16)
        two = jnp.where(lanes >= 64, wide, 0.0).astype(BF16)
        return jnp.concatenate([one, two], axis=0)

    def decay_pairs(first, count):
        causal = lax.broadcasted_iota(jnp.int32, (rows, rows), 0) >= lax.broadcasted_iota(
            jnp.int32, (rows, rows), 1
        )

        def one_pair(k, carry):
            at = pl.multiple_of(k * 128, 128)
            both = split_heads(x[:, pl.ds(at, 128)])
            outer = dot(g[:, pl.ds(at, 128)], both, NT)
            total = jnp.zeros((rows, rows), F32)
            for i in range(2):
                head = 2 * k + i
                along = jnp.broadcast_to(tot[pl.ds(head, 1), :], (rows, rows))
                spread = jnp.where(causal, along.T - along, -1e30)
                factor = jnp.exp(spread) * step_ref[pl.ds(head, 1), :]
                decay[head] = factor
                total += factor * outer[:, i * 128 : (i + 1) * 128]
            score_grad[k // grp_pairs] += total
            return carry

        lax.fori_loop(first, first + count, one_pair, 0)

    base = ((f * 4) + y) * 2
    for j in range(2):
        got(listed.at[j], LIST_ + j)

    def picked(j, k):
        return (listed[j, j : j + 1, :] == base + k).astype(F32)

    load_a.wait()
    load_b.wait()
    for j in range(2):
        m0, m1 = picked(j, 0), picked(j, 1)
        for zc in range(NZ):
            for i in range(5):
                src, at = (a_own, zc * 512 + i * 128) if i < 4 else (b_own, zc * 128)
                value = (
                    src[0, :, at : at + 128].astype(F32) * m0
                    + src[1, :, at : at + 128].astype(F32) * m1
                )
                cand[j, zc, :, i * 128 : (i + 1) * 128] = value.astype(BF16)
    send(cand.at[1 - c], rcore, FCORE, sib)

    got(piece(0, 1, p), X_)
    for way in range(2):
        send(piece(0, 1, p), piece(0, 1, p), Z_ + way * 8 + 4, zdev(1 - 2 * way))

    def zstep(s):
        for way, which, last in ((0, 0, 4), (1, 0, 3), (1, 1, 4), (0, 1, 3)):
            if s > last:
                continue
            d = -s if way == 0 else s
            slot = Z_ + way * 8 + which * 4 + s - 1
            part_in = piece(d, which, p)
            got(part_in, slot)
            if s < last:
                send(part_in, part_in, slot + 1, zdev(1 - 2 * way))
            send(part_in, part_in, Y_ + which * 8 + d % 8, ydev(1 if which == 0 else -1))

    def offsets(s):
        return (0,) if s == 0 else (4,) if s == 4 else (-s, s)

    def ystep(s):
        for d in offsets(s):
            for which in range(2):
                got(piece(d, which, 1 - p), Y_ + which * 8 + d % 8)
                send(whole(d, which, c), whole(d, which, c), D_ + which * 8 + d % 8, sib)

    def forward(s):
        for d in offsets(s):
            for which in range(2):
                got(whole(d, which, 1 - c), D_ + which * 8 + d % 8)
        for d in offsets(s):
            at = zat(d)

            def part_n(n, carry, at=at, first=s == 0):
                cols = pl.ds(pl.multiple_of(n * 256, 256), 256)
                value = dot(tok[:, pl.ds(pl.multiple_of(at * 1024, 1024), 1024)], w[at, :, cols])
                if first:
                    acc[:, cols] = value
                else:
                    acc[:, cols] += value
                return carry

            lax.fori_loop(0, 4, part_n, 0)

    quarter = pairs // 4
    decay_pairs(0, quarter)
    got(piece(0, 1, 1 - p), X_ + 1)
    send(whole(0, 1, c), whole(0, 1, c), D_ + 8, sib)
    zstep(1)

    got(rcore, FCORE)
    cand[c] = cand[c] + rcore[...]
    mine = pl.ds(pl.multiple_of(32 * l, 32), 32)
    other = pl.ds(pl.multiple_of(32 * (1 - l), 32), 32)
    send(cand.at[c, :, other, :], rx, FX, xdev)
    decay_pairs(quarter, quarter)
    load_tok.wait()
    forward(0)
    zstep(2)
    ystep(1)
    got(rx, FX)
    rx[...] = rx[...] + cand[c, :, mine, :]
    for d in range(1, NZ):
        send(rx.at[zat(d)], rz.at[d], FZ_ + d, zdev(d))
    decay_pairs(2 * quarter, quarter)
    forward(1)
    zstep(3)
    ystep(2)
    total = rx[z].astype(F32)
    for d in range(1, NZ):
        got(rz.at[d], FZ_ + d)
        total += rz[d].astype(F32)
    chunk[...] = total.astype(BF16)
    send(chunk, ry, FY, ydev(2 + c))
    decay_pairs(3 * quarter, quarter)
    forward(2)
    got(ry, FY)
    full[c, z, mine, :] = ry[...]
    for d in range(1, NZ):
        send(ry, full.at[c, z, mine, :], GZ_ + d, zdev(d))
    zstep(4)
    ystep(3)
    for d in range(1, NZ):
        got(full.at[c, zat(-d), mine, :], GZ_ + d)
    send(full.at[c, :, mine, :], full.at[c, :, mine, :], GX, xdev)
    forward(3)
    got(full.at[c, :, other, :], GX)
    send(full.at[c], full.at[c], GCORE, sib)
    ystep(4)
    got(full.at[1 - c], GCORE)
    slot = slot_ref[0]
    half = pl.multiple_of(t * 4096, 4096)
    low_part = jnp.zeros((64, rows), F32)
    for zc in range(NZ):
        piece_ab = full[slot, zc]
        sel_a[:, zc * 512 : (zc + 1) * 512] = piece_ab[:, :512]
        sel_b[:, zc * 128 : (zc + 1) * 128] = piece_ab[:, 512:]
        low_part += dot(piece_ab[:, :512], tok[:, pl.ds(half + zc * 512, 512)], NT)
    low_s[...] = low_part
    send(low_s, low_r, LOW, tdev)
    forward(4)
    got(low_r, LOW)
    low_t[...] = (low_s[...] + low_r[...]).astype(BF16)
    proj[...] = (acc[...] + dot(low_t[...], sel_b[...], TN)).astype(BF16)

    scores = []
    for gi in range(2):
        b_in = proj[:, gi * 512 : gi * 512 + 256]
        c_out = proj[:, gi * 512 + 256 : gi * 512 + 512]
        scores.append(dot(c_out, b_in, NT))
        sg = score_grad[gi].astype(BF16)
        gproj[:, gi * 512 : gi * 512 + 256] = dot(sg, c_out, TN).astype(BF16)
        gproj[:, gi * 512 + 256 : gi * 512 + 512] = dot(sg, b_in).astype(BF16)
    q_s[...] = dot(sel_b[...], gproj[...], NT)
    send(q_s, q_r, Q, tdev)
    for gi in range(2):
        score_grad[gi] = scores[gi]

    def back(at, n):
        return dot(gproj[...], w[at, pl.ds(pl.multiple_of(n * 256, 256), 256), :], NT)

    for k in range(4):

        def partner_n(n, carry, k=k):
            cols = pl.ds(pl.multiple_of(n * 256, 256), 256)
            psend[k, :, cols] = back(4 * (1 - t) + k, n).astype(BF16)
            return carry

        lax.fori_loop(0, 4, partner_n, 0)
        send(psend.at[k], precv.at[k], PIN_ + k, tdev)

    got(q_r, Q)
    q_t[...] = (q_s[...] + q_r[...]).astype(BF16)
    for zc in range(NZ):
        ga = dot(q_t[...], tok[:, pl.ds(half + zc * 512, 512)])
        gb = dot(low_t[...], gproj[:, zc * 128 : (zc + 1) * 128])
        for j in range(2):
            chosen = jnp.where(slot == j, 1.0, 0.0).astype(F32)
            bcand[j, zc, :, :512] = (ga * chosen).astype(BF16)
            bcand[j, zc, :, 512:] = (gb * chosen).astype(BF16)
    send(bcand.at[1 - c], brcore, BCORE, sib)

    def own_n(n, carry):
        cols = pl.ds(pl.multiple_of(n * 256, 256), 256)
        part[:, cols] = back(4 * t + n // 4, n % 4) + dot(q_t[...], sel_a[:, cols], TN)
        return carry

    lax.fori_loop(0, 16, own_n, 0)

    got(brcore, BCORE)
    for zc in range(NZ):
        bcand[c, zc] = (bcand[c, zc].astype(F32) + brcore[zc].astype(F32)).astype(BF16)
    for d in range(1, NZ):
        send(bcand.at[c, zat(d)], brz.at[d], BZ_ + d, zdev(d))

    def mix_pair(k, carry):
        at = pl.multiple_of(k * 128, 128)
        both = split_heads(x[:, pl.ds(at, 128)])
        score = score_grad[k // grp_pairs]
        weight = jnp.concatenate(
            [(decay[2 * k] * score).astype(BF16), (decay[2 * k + 1] * score).astype(BF16)], axis=1
        )
        mixed[:, pl.ds(at, 128)] = dot(weight, both).astype(BF16)
        return carry

    lax.fori_loop(0, pairs, mix_pair, 0)
    out_mixed = local(mixed, mixed_hbm, 6)

    total = bcand[c, z].astype(F32)
    for d in range(1, NZ):
        got(brz.at[d], BZ_ + d)
        total += brz[d].astype(F32)
    bs[...] = total.astype(BF16)
    send(bs.at[other, :], brx, BX, xdev)
    got(brx, BX)
    bchunk[...] = (bs[mine, :].astype(F32) + brx[...].astype(F32)).astype(BF16)
    send(bchunk, bry, BY, ydev(2 - c))
    got(bry, BY)
    bfull[c, z, mine, :] = bry[...]
    send(bry, bfull.at[c, z, mine, :], HX, xdev)
    got(bfull.at[c, z, other, :], HX)
    for d in range(1, NZ):
        send(bfull.at[c, z], bfull.at[c, z], HZ_ + d, zdev(d))

    for k in range(4):
        got(precv.at[k], PIN_ + k)
        cols = slice(k * 1024, (k + 1) * 1024)
        igrad[:, cols] = (part[:, cols] + precv[k].astype(F32)).astype(BF16)
    out_igrad = local(igrad, igrad_hbm, 7)

    for d in range(1, NZ):
        got(bfull.at[c, zat(-d)], HZ_ + d)
    send(bfull.at[c], bfull.at[c], HCORE, sib)
    got(bfull.at[1 - c], HCORE)
    for k in range(2):
        m0, m1 = picked(0, k), picked(1, k)
        for zc in range(NZ):
            for i in range(5):
                dst, at = (agrad, zc * 512 + i * 128) if i < 4 else (bgrad, zc * 128)
                lane = slice(i * 128, (i + 1) * 128)
                value = (
                    bfull[0, zc, :, lane].astype(F32) * m0 + bfull[1, zc, :, lane].astype(F32) * m1
                )
                dst[k, :, at : at + 128] = value.astype(BF16)
    out_a = local(agrad, agrad_hbm, 8)
    out_b = local(bgrad, bgrad_hbm, 9)
    for copy in sent:
        copy.wait_send()
    for copy in (out_mixed, out_igrad, out_a, out_b):
        copy.wait()


def shards(
    tokens, inner_x, step_size, decay_rate, grad_out, w_bc,
    a_store, b_store, tenant_list, block_slot, owner_slot,
):
    rows = tokens.shape[0]
    heads = decay_rate.shape[0]
    location = owner_slot[tenant_list[0]]
    loc = jnp.broadcast_to(jnp.pad(location, (0, 6))[:, None], (8, 128))
    a_t = jnp.swapaxes(a_store, 1, 2)
    half = inner_x.shape[1]
    cols = w_bc.shape[1]
    rate = jnp.broadcast_to(decay_rate[:, None], (heads, rows))
    hbm = pl.BlockSpec(memory_space=pl.ANY)
    vmem = pl.BlockSpec(memory_space=pltpu.VMEM)
    smem = pl.BlockSpec(memory_space=pltpu.SMEM)
    mixed, igrad, agrad, bgrad = pl.pallas_call(
        body,
        out_shape=(
            jax.ShapeDtypeStruct((rows, half), BF16),
            jax.ShapeDtypeStruct((rows, half), BF16),
            jax.ShapeDtypeStruct(a_t.shape, BF16),
            jax.ShapeDtypeStruct(b_store.shape, BF16),
        ),
        in_specs=[smem, hbm, hbm, vmem, vmem, hbm, hbm, hbm, hbm, vmem],
        out_specs=(hbm, hbm, hbm, hbm),
        scratch_shapes=[
            pltpu.VMEM((NZ, 1024, cols), BF16),
            pltpu.VMEM(tokens.shape, BF16),
            pltpu.VMEM((rows, half), BF16),
            pltpu.VMEM((rows, half), BF16),
            pltpu.VMEM(a_t.shape, BF16),
            pltpu.VMEM(b_store.shape, BF16),
            pltpu.VMEM((2, 8, 128), jnp.int32),
            pltpu.VMEM((2, NZ, 64, 640), BF16),
            pltpu.VMEM((NZ, 64, 640), BF16),
            pltpu.VMEM((NZ, 32, 640), BF16),
            pltpu.VMEM((NZ, 32, 640), BF16),
            pltpu.VMEM((32, 640), BF16),
            pltpu.VMEM((32, 640), BF16),
            pltpu.VMEM((2, NZ, 64, 640), BF16),
            pltpu.VMEM((64, half), BF16),
            pltpu.VMEM((64, cols), BF16),
            pltpu.VMEM((64, rows), F32),
            pltpu.VMEM((64, rows), F32),
            pltpu.VMEM((64, rows), BF16),
            pltpu.VMEM((heads, rows, rows), F32),
            pltpu.VMEM((heads, rows), F32),
            pltpu.VMEM((2, rows, rows), F32),
            pltpu.VMEM((rows, cols), F32),
            pltpu.VMEM((rows, cols), BF16),
            pltpu.VMEM((rows, cols), BF16),
            pltpu.VMEM((64, rows), F32),
            pltpu.VMEM((64, rows), F32),
            pltpu.VMEM((64, rows), BF16),
            pltpu.VMEM((4, rows, 1024), BF16),
            pltpu.VMEM((4, rows, 1024), BF16),
            pltpu.VMEM((rows, half), F32),
            pltpu.VMEM((rows, half), BF16),
            pltpu.VMEM((rows, half), BF16),
            pltpu.VMEM((2, NZ, 64, 640), BF16),
            pltpu.VMEM((NZ, 64, 640), BF16),
            pltpu.VMEM((NZ, 64, 640), BF16),
            pltpu.VMEM((64, 640), BF16),
            pltpu.VMEM((32, 640), BF16),
            pltpu.VMEM((32, 640), BF16),
            pltpu.VMEM((32, 640), BF16),
            pltpu.VMEM((2, NZ, 64, 640), BF16),
            pltpu.VMEM(a_t.shape, BF16),
            pltpu.VMEM(b_store.shape, BF16),
            pltpu.SemaphoreType.DMA((SLOTS,)),
            pltpu.SemaphoreType.DMA((SLOTS,)),
            pltpu.SemaphoreType.DMA((10,)),
        ],
        compiler_params=pltpu.CompilerParams(
            collective_id=0, has_side_effects=True, vmem_limit_bytes=56 * 1024 * 1024
        ),
    )(block_slot, tokens, inner_x, step_size.T, rate, grad_out, w_bc, a_t, b_store, loc)
    return mixed, igrad, jnp.swapaxes(agrad, 1, 2), bgrad


def solution(mesh):
    both = ("fsdp", "tenant")
    placed = (
        P(both, None),
        P(both, "tensor"),
        P(both, "tensor"),
        P("tensor"),
        P(both, "tensor"),
        P("fsdp", "tensor"),
        P(both, "tensor", None),
        P(both, None, "tensor"),
        P("tenant", None),
        P(both),
        P(),
    )
    return jax.shard_map(
        shards,
        mesh=mesh,
        in_specs=placed,
        out_specs=(
            P(both, "tensor"),
            P(both, "tensor"),
            P(both, "tensor", None),
            P(both, None, "tensor"),
        ),
        check_vma=False,
    )
```

time: 698 us -> 147 us (0.21)
  waiting for transfers between devices: 453 us -> 0 us
  blocking collectives: 156 us -> 0 us
  Pallas kernels: 0 us -> 136 us
  matrix products: 44 us -> 0 us
  between operations: 20.3 us -> 1.33 us
  other arithmetic: 8.8 us -> 0.67 us
  local copies, waits for them, and re-layouts: 15.1 us -> 7.75 us
    psum x1 -> x0, waiting for transfers between devices: 223 us -> none  [spread_2(): return lax.psum(block, axis)]
    all_gather x3 -> x0, waiting for transfers between devices: 166 us -> none  [the longest x1 91.7 us: shards(): whole_w = lax.all_gather(w_bc, 'fsdp', axis=0, tiled=True)]
    psum x3 -> x0, blocking collectives: 156 us -> none  [the longest x1 137 us: shards(): group_a, group_b = lax.psum((list_grad_a, list_grad_b), 'fsdp')]
    pallas_call x0 -> x1, Pallas kernels: none -> 136 us  [shards(): pl.pallas_call(body, out_shape=(jax.ShapeDtypeStruct((rows, half), BF16),...]
    reduce_scatter x3 -> x0, waiting for transfers between devices: 62.5 us -> none  [the longest x1 54.3 us: shards(): lax.psum_scatter(send_a.astype(jnp.bfloat16), 'tenant', scatter_dimension...]
    dot_general x15 -> x0, matrix products: 44 us -> none  [the longest x1 13.5 us: shards(): jnp.dot(grad_proj, whole_w.T, preferred_element_type=jnp.float32)]
  transfers between devices with their start and end apart: 7 -> 0, of which waited for: 6 -> 0; matrix products, arithmetic and copies ran while one was open for 6% -> 0% of each run, Pallas kernels for 0% -> 0%
where the time goes in v1:
time: 147 us; the launch traced here: 146 us
  Pallas kernels  136 us (93%)
  local copies, waits for them, and re-layouts  7.75 us (5%)
    pallas_call x1, Pallas kernels, shards(): pl.pallas_call(body, out_shape=(jax.ShapeDtypeStruct((rows, half), BF16),...  136 us
    unnamed x12, local copies, waits for them, and re-layouts  5.1 us

profile of v1, /device:TPU:1, one launch (start us, length us, event | category | flops | bytes accessed | tf_op | source)
XLA Modules:
  0.0 146.1 jit_solution(5438935763153994250)
XLA Ops:
  0.6 0.0 copy-start
  1.3 0.7 fusion
  2.0 0.0 copy-done
  2.0 0.6 gather_fusion
  2.6 0.7 broadcast_in_dim.5.loc_ref
  3.3 1.3 broadcast_in_dim.4.rate_ref
  4.6 136.4 %shard_map.138 = (bf16[128,4096]{1,0:T(8,128)(2,1)}, bf16[128,4096]{1,0:T(8,128)(2,1)}, bf16[2,64,4096]{2,1,0:T(8,128)(2,1)}, bf16[2,64,1024]{2,1,0:T(8,128)(2,1)}) custom-call(s32[1]{0:T(128)S(6)} %copy.19.slot_ref, bf16[128,8192]{1,0:T(8,128)(2,1)} %tok_hbm.1, bf16[128,4096]{1,0:T(8,128)(2,1)} %x_hbm.1, f32[64,128]{1,0:T(8,128)} %bitcast.9, ...), custom_call_target="tpu_custom_call" | custom-call | tf_op jit(solution)/shard_map/pallas_call | solution.py:402
  141.0 0.0 copy-start.2
  141.0 0.0 copy-start.1
  141.0 2.4 %copy.20 = bf16[128,4096]{1,0:T(8,128)(2,1)} copy(bf16[128,4096]{1,0:T(8,128)(2,1)} %get-tuple-element.16) | data formatting | bytes 2097152
  143.5 0.0 copy-done.2
  143.5 0.0 copy-start.3
  143.5 1.0 copy.21
  144.4 0.0 copy-done.1
  144.4 1.0 copy.22
  145.4 0.0 copy-done.3
  145.4 0.7 copy.23
  (2 shorter events, 0.0 us)
Async XLA Ops:
  0.6 1.3 copy-start
  141.0 2.5 %copy-start.2 = (bf16[128,4096]{1,0:T(8,128)(2,1)S(1)}, bf16[128,4096]{1,0:T(8,128)(2,1)}, u32[]{:S(2)}) copy-start(bf16[128,4096]{1,0:T(8,128)(2,1)} %get-tuple-element.17) | copy-start | bytes 3145732
  141.0 3.4 %copy-start.1 = (bf16[2,64,4096]{2,1,0:T(8,128)(2,1)S(1)}, bf16[2,64,4096]{2,1,0:T(8,128)(2,1)}, u32[]{:S(2)}) copy-start(bf16[2,64,4096]{2,1,0:T(8,128)(2,1)} %get-tuple-element.10) | copy-start | bytes 3145732
  143.5 1.9 %copy-start.3 = (bf16[2,64,1024]{2,1,0:T(8,128)(2,1)S(1)}, bf16[2,64,1024]{2,1,0:T(8,128)(2,1)}, u32[]{:S(2)}) copy-start(bf16[2,64,1024]{2,1,0:T(8,128)(2,1)} %get-tuple-element.19) | copy-start | bytes 786436

commit v2 on v1

--- a/solution.py
+++ b/solution.py
@@ -12,10 +12,11 @@
 HEADS_GRP = 32
 NS = 256
 
-X_, Z_, Y_, D_ = 0, 2, 18, 34
-LIST_, FCORE, FX, FZ_, FY, GZ_, GX, GCORE, LOW = 50, 52, 53, 54, 62, 63, 71, 72, 73
-Q, PIN_, BCORE, BZ_, BX, BY, HX, HZ_, HCORE = 74, 75, 79, 80, 88, 89, 90, 91, 99
-SLOTS = 100
+X_, Z_, Y_, D_, XR = 0, 4, 36, 68, 84
+LIST_, LOW, Q, PIN_ = 88, 90, 91, 92
+CORE, ACROSS, Z1, Z2, OVER, GZ, GX, GC = 0, 1, 2, 5, 9, 10, 18, 26
+FETCH, BACK = 96, 130
+SLOTS = 164
 
 NN = (((1,), (0,)), ((), ()))
 NT = (((1,), (1,)), ((), ()))
@@ -27,12 +28,12 @@
 
 
 def body(
-    slot_ref, tok_hbm, x_hbm, step_ref, rate_ref, g_hbm, w_hbm, a_hbm, b_hbm, loc_ref,
+    slot_ref, list_ref, owner_ref, rate_ref, step_ref, tok_hbm, x_hbm, g_hbm, w_hbm, a_hbm, b_hbm,
     mixed_hbm, igrad_hbm, agrad_hbm, bgrad_hbm,
-    w, tok, x, g, a_own, b_own, listed, cand, rcore, rx, rz, chunk, ry, full,
+    w, tok, x, g, a_own, b_own, loc, listed, cand, rcore, rx, r1, r2, chunk, full,
     sel_a, sel_b, low_s, low_r, low_t, decay, tot, score_grad, acc, proj, gproj,
     q_s, q_r, q_t, psend, precv, part, mixed, igrad,
-    bcand, brcore, brz, bs, brx, bchunk, bry, bfull, agrad, bgrad,
+    bcand, brcore, br1, br2, bs, brx, bchunk, bfull, agrad, bgrad,
     ssem, rsem, lsem,
 ):
     f = lax.axis_index("fsdp")
@@ -83,9 +84,12 @@
     def lside(which):
         return l if which == 0 else 1 - l
 
-    def piece(d, which, par):
-        first = pl.multiple_of((lside(which) * 2 + c) * 256 + par * 128, 128)
-        return w.at[zat(d), pl.ds(first, 128), :]
+    def piece(d, which, par, h):
+        first = pl.multiple_of((lside(which) * 2 + c) * 256 + par * 128 + h * 64, 64)
+        return w.at[zat(d), pl.ds(first, 64), :]
+
+    def move(part, slot, dev):
+        send(part, part, slot, dev)
 
     def whole(d, which, core):
         first = pl.multiple_of((lside(which) * 2 + core) * 256, 256)
@@ -104,21 +108,27 @@
         pl.semaphore_signal(barrier, inc=1, device_id=dev, device_id_type=MESH)
     pl.semaphore_wait(barrier, len(partners))
 
+    loc[...] = jnp.where(
+        lax.broadcasted_iota(jnp.int32, loc.shape, 0) == 0,
+        owner_ref[list_ref[0, 0]],
+        owner_ref[list_ref[0, 1]],
+    )
     for j in range(2):
-        send(loc_ref, listed.at[j], LIST_ + j, ydev(2 - j))
+        send(loc, listed.at[j], LIST_ + j, ydev(2 - j))
     load_w.wait()
-    send(piece(0, 0, p), piece(0, 0, p), X_, xdev)
-    for way in range(2):
-        send(piece(0, 0, p), piece(0, 0, p), Z_ + way * 8, zdev(1 - 2 * way))
-    send(piece(0, 0, 1 - p), piece(0, 0, 1 - p), X_ + 1, xdev)
+    for h in range(2):
+        move(piece(0, 0, p, h), X_ + h, xdev)
+        for way in range(2):
+            move(piece(0, 0, p, h), Z_ + way * 16 + h, zdev(1 - 2 * way))
     send(whole(0, 0, c), whole(0, 0, c), D_, sib)
 
     upto = (
         lax.broadcasted_iota(jnp.int32, (rows, rows), 0)
         <= lax.broadcasted_iota(jnp.int32, (rows, rows), 1)
     ).astype(F32)
-    tot[...] = dot(-step_ref[...] * rate_ref[...], upto, precision=lax.Precision.HIGHEST)
+    tot[...] = dot(-step_ref[...], upto, precision=lax.Precision.HIGHEST)
     score_grad[...] = jnp.zeros_like(score_grad)
+    acc[...] = jnp.zeros_like(acc)
     load_x.wait()
     load_g.wait()
 
@@ -142,7 +152,7 @@
             total = jnp.zeros((rows, rows), F32)
             for i in range(2):
                 head = 2 * k + i
-                along = jnp.broadcast_to(tot[pl.ds(head, 1), :], (rows, rows))
+                along = jnp.broadcast_to(tot[pl.ds(head, 1), :] * rate_ref[head], (rows, rows))
                 spread = jnp.where(causal, along.T - along, -1e30)
                 factor = jnp.exp(spread) * step_ref[pl.ds(head, 1), :]
                 decay[head] = factor
@@ -171,23 +181,80 @@
                     + src[1, :, at : at + 128].astype(F32) * m1
                 )
                 cand[j, zc, :, i * 128 : (i + 1) * 128] = value.astype(BF16)
-    send(cand.at[1 - c], rcore, FCORE, sib)
-
-    got(piece(0, 1, p), X_)
-    for way in range(2):
-        send(piece(0, 1, p), piece(0, 1, p), Z_ + way * 8 + 4, zdev(1 - 2 * way))
-
-    def zstep(s):
-        for way, which, last in ((0, 0, 4), (1, 0, 3), (1, 1, 4), (0, 1, 3)):
-            if s > last:
-                continue
-            d = -s if way == 0 else s
-            slot = Z_ + way * 8 + which * 4 + s - 1
-            part_in = piece(d, which, p)
-            got(part_in, slot)
-            if s < last:
-                send(part_in, part_in, slot + 1, zdev(1 - 2 * way))
-            send(part_in, part_in, Y_ + which * 8 + d % 8, ydev(1 if which == 0 else -1))
+    send(cand.at[1 - c], rcore, FETCH + CORE, sib)
+    mine = pl.ds(pl.multiple_of(32 * l, 32), 32)
+    other = pl.ds(pl.multiple_of(32 * (1 - l), 32), 32)
+
+    def reduce_start(own, one, two, at):
+        send(own(3), one.at[0], at + Z1, zdev(1))
+        send(own(4), one.at[1], at + Z1 + 1, zdev(2))
+        send(own(-3), one.at[2], at + Z1 + 2, zdev(-1))
+        send(own(1), two.at[0], at + Z2, zdev(1))
+        send(own(-1), two.at[1], at + Z2 + 1, zdev(-1))
+
+    def reduce_relay(own, one, two, at):
+        for i in range(3):
+            got(one.at[i], at + Z1 + i)
+        up = one[0].astype(F32) + one[1].astype(F32) + own(2)[...].astype(F32)
+        one[0] = up.astype(BF16)
+        send(one.at[0], two.at[2], at + Z2 + 2, zdev(2))
+        one[2] = (one[2].astype(F32) + own(-2)[...].astype(F32)).astype(BF16)
+        send(one.at[2], two.at[3], at + Z2 + 3, zdev(-2))
+
+    def reduce_end(own, two, at):
+        total = own(0)[...].astype(F32)
+        for i in range(4):
+            got(two.at[i], at + Z2 + i)
+            total += two[i].astype(F32)
+        return total
+
+    def held(buf, d, wide):
+        return buf.at[c, zat(-d)] if wide else buf.at[c, zat(-d), mine, :]
+
+    def gather_start(buf, at, wide):
+        own = held(buf, 0, wide)
+        for d in (2, -2, 1, -1):
+            move(own, at + GZ + d % 8, zdev(d))
+        move(own, at + (GC if wide else GX), sib if wide else xdev)
+
+    def gather_in(buf, at, wide, d, hops=()):
+        here = held(buf, d, wide)
+        got(here, at + GZ + d % 8)
+        for hop in hops:
+            move(here, at + GZ + (d + hop) % 8, zdev(hop))
+        move(here, at + (GC if wide else GX) + d % 8, sib if wide else xdev)
+
+    def gather_core(buf, at, offs):
+        for d in offs:
+            got(buf.at[c, zat(-d), other, :], at + GX + d % 8)
+            send(buf.at[c, zat(-d)], buf.at[c, zat(-d)], at + GC + d % 8, sib)
+
+    def gather_end(buf, at):
+        for d in range(NZ):
+            got(buf.at[1 - c, zat(-d)], at + GC + d)
+
+
+    def zstep(s, side):
+        for h in range(2):
+            for way, which, last in ((0, 0, 4), (1, 0, 2), (1, 1, 4), (0, 1, 2)):
+                if s > last or which != side:
+                    continue
+                d = -s if way == 0 else s
+                slot = Z_ + way * 16 + which * 8 + (s - 1) * 2 + h
+                part_in = piece(d, which, p, h)
+                got(part_in, slot)
+                if s < last:
+                    move(part_in, slot + 2, zdev(1 - 2 * way))
+                move(part_in, Y_ + which * 16 + d % 8 * 2 + h, ydev(1 if which == 0 else -1))
+                if s == 3:
+                    move(part_in, XR + way * 2 + h, xdev)
+
+    def xstep(way):
+        d, which = (-3, 1) if way == 0 else (3, 0)
+        for h in range(2):
+            part_in = piece(d, which, p, h)
+            got(part_in, XR + way * 2 + h)
+            move(part_in, Y_ + which * 16 + d % 8 * 2 + h, ydev(1 if which == 0 else -1))
 
     def offsets(s):
         return (0,) if s == 0 else (4,) if s == 4 else (-s, s)
@@ -195,7 +262,8 @@
     def ystep(s):
         for d in offsets(s):
             for which in range(2):
-                got(piece(d, which, 1 - p), Y_ + which * 8 + d % 8)
+                for h in range(2):
+                    got(piece(d, which, 1 - p, h), Y_ + which * 16 + d % 8 * 2 + h)
                 send(whole(d, which, c), whole(d, which, c), D_ + which * 8 + d % 8, sib)
 
     def forward(s):
@@ -205,63 +273,69 @@
         for d in offsets(s):
             at = zat(d)
 
-            def part_n(n, carry, at=at, first=s == 0):
+            def part_n(n, carry, at=at):
                 cols = pl.ds(pl.multiple_of(n * 256, 256), 256)
-                value = dot(tok[:, pl.ds(pl.multiple_of(at * 1024, 1024), 1024)], w[at, :, cols])
-                if first:
-                    acc[:, cols] = value
-                else:
-                    acc[:, cols] += value
+                acc[:, cols] += dot(
+                    tok[:, pl.ds(pl.multiple_of(at * 1024, 1024), 1024)], w[at, :, cols]
+                )
                 return carry
 
             lax.fori_loop(0, 4, part_n, 0)
 
     quarter = pairs // 4
-    decay_pairs(0, quarter)
-    got(piece(0, 1, 1 - p), X_ + 1)
+
+    def own_rows(k):
+        return rx.at[zat(k)]
+
+    for h in range(2):
+        got(piece(0, 1, p, h), X_ + h)
+        for way in range(2):
+            move(piece(0, 1, p, h), Z_ + way * 16 + 8 + h, zdev(1 - 2 * way))
+    got(rcore, FETCH + CORE)
+    cand[c] = cand[c] + rcore[...]
+    send(cand.at[c, :, other, :], rx, FETCH + ACROSS, xdev)
+    zstep(1, 0)
+    zstep(1, 1)
+    decay_pairs(0, quarter * 2)
+    got(rx, FETCH + ACROSS)
+    rx[...] = rx[...] + cand[c, :, mine, :]
+    reduce_start(own_rows, r1, r2, FETCH)
+    zstep(2, 0)
+    for h in range(2):
+        move(piece(0, 0, 1 - p, h), X_ + 2 + h, xdev)
+    decay_pairs(quarter * 2, quarter)
+    ystep(1)
+    zstep(2, 1)
+    load_tok.wait()
+    forward(1)
+    reduce_relay(own_rows, r1, r2, FETCH)
+    zstep(3, 0)
+    zstep(3, 1)
+    chunk[...] = reduce_end(own_rows, r2, FETCH).astype(BF16)
+    send(chunk, full.at[c, z, mine, :], FETCH + OVER, ydev(2 + c))
+    for h in range(2):
+        got(piece(0, 1, 1 - p, h), X_ + 2 + h)
     send(whole(0, 1, c), whole(0, 1, c), D_ + 8, sib)
-    zstep(1)
-
-    got(rcore, FCORE)
-    cand[c] = cand[c] + rcore[...]
-    mine = pl.ds(pl.multiple_of(32 * l, 32), 32)
-    other = pl.ds(pl.multiple_of(32 * (1 - l), 32), 32)
-    send(cand.at[c, :, other, :], rx, FX, xdev)
-    decay_pairs(quarter, quarter)
-    load_tok.wait()
+    ystep(2)
+    decay_pairs(quarter * 3, quarter // 2)
+    xstep(0)
     forward(0)
-    zstep(2)
-    ystep(1)
-    got(rx, FX)
-    rx[...] = rx[...] + cand[c, :, mine, :]
-    for d in range(1, NZ):
-        send(rx.at[zat(d)], rz.at[d], FZ_ + d, zdev(d))
-    decay_pairs(2 * quarter, quarter)
-    forward(1)
-    zstep(3)
-    ystep(2)
-    total = rx[z].astype(F32)
-    for d in range(1, NZ):
-        got(rz.at[d], FZ_ + d)
-        total += rz[d].astype(F32)
-    chunk[...] = total.astype(BF16)
-    send(chunk, ry, FY, ydev(2 + c))
-    decay_pairs(3 * quarter, quarter)
+    got(full.at[c, z, mine, :], FETCH + OVER)
+    gather_start(full, FETCH, False)
+    zstep(4, 1)
+    xstep(1)
+    gather_in(full, FETCH, False, 2, (1, 2))
+    gather_in(full, FETCH, False, -2, (-1,))
+    zstep(4, 0)
     forward(2)
-    got(ry, FY)
-    full[c, z, mine, :] = ry[...]
-    for d in range(1, NZ):
-        send(ry, full.at[c, z, mine, :], GZ_ + d, zdev(d))
-    zstep(4)
     ystep(3)
-    for d in range(1, NZ):
-        got(full.at[c, zat(-d), mine, :], GZ_ + d)
-    send(full.at[c, :, mine, :], full.at[c, :, mine, :], GX, xdev)
+    for d in (1, -1, 3, -3, 4):
+        gather_in(full, FETCH, False, d)
+    decay_pairs(quarter * 3 + quarter // 2, quarter // 2)
     forward(3)
-    got(full.at[c, :, other, :], GX)
-    send(full.at[c], full.at[c], GCORE, sib)
+    gather_core(full, FETCH, (0, 2, -2, 1, -1, 3, -3, 4))
     ystep(4)
-    got(full.at[1 - c], GCORE)
+    gather_end(full, FETCH)
     slot = slot_ref[0]
     half = pl.multiple_of(t * 4096, 4096)
     low_part = jnp.zeros((64, rows), F32)
@@ -293,15 +367,19 @@
     def back(at, n):
         return dot(gproj[...], w[at, pl.ds(pl.multiple_of(n * 256, 256), 256), :], NT)
 
-    for k in range(4):
-
-        def partner_n(n, carry, k=k):
+    def partner(k):
+        def partner_n(n, carry):
             cols = pl.ds(pl.multiple_of(n * 256, 256), 256)
             psend[k, :, cols] = back(4 * (1 - t) + k, n).astype(BF16)
             return carry
 
         lax.fori_loop(0, 4, partner_n, 0)
+
+    def to_partner(k):
         send(psend.at[k], precv.at[k], PIN_ + k, tdev)
+
+    partner(0)
+    to_partner(0)
 
     got(q_r, Q)
     q_t[...] = (q_s[...] + q_r[...]).astype(BF16)
@@ -312,20 +390,27 @@
             chosen = jnp.where(slot == j, 1.0, 0.0).astype(F32)
             bcand[j, zc, :, :512] = (ga * chosen).astype(BF16)
             bcand[j, zc, :, 512:] = (gb * chosen).astype(BF16)
-    send(bcand.at[1 - c], brcore, BCORE, sib)
+    send(bcand.at[1 - c], brcore, BACK + CORE, sib)
+    partner(1)
+    to_partner(1)
 
     def own_n(n, carry):
         cols = pl.ds(pl.multiple_of(n * 256, 256), 256)
         part[:, cols] = back(4 * t + n // 4, n % 4) + dot(q_t[...], sel_a[:, cols], TN)
         return carry
 
-    lax.fori_loop(0, 16, own_n, 0)
-
-    got(brcore, BCORE)
+    def own_sum(k):
+        return bcand.at[c, zat(k)]
+
+    got(brcore, BACK + CORE)
     for zc in range(NZ):
         bcand[c, zc] = (bcand[c, zc].astype(F32) + brcore[zc].astype(F32)).astype(BF16)
-    for d in range(1, NZ):
-        send(bcand.at[c, zat(d)], brz.at[d], BZ_ + d, zdev(d))
+    reduce_start(own_sum, br1, br2, BACK)
+    partner(2)
+    partner(3)
+    lax.fori_loop(0, 5, own_n, 0)
+    reduce_relay(own_sum, br1, br2, BACK)
+    lax.fori_loop(5, 16, own_n, 0)
 
     def mix_pair(k, carry):
         at = pl.multiple_of(k * 128, 128)
@@ -337,35 +422,33 @@
         mixed[:, pl.ds(at, 128)] = dot(weight, both).astype(BF16)
         return carry
 
-    lax.fori_loop(0, pairs, mix_pair, 0)
+    bs[...] = reduce_end(own_sum, br2, BACK).astype(BF16)
+    send(bs.at[other, :], brx, BACK + ACROSS, xdev)
+    got(brx, BACK + ACROSS)
+    bchunk[...] = (bs[mine, :].astype(F32) + brx[...].astype(F32)).astype(BF16)
+    send(bchunk, bfull.at[c, z, mine, :], BACK + OVER, ydev(2 - c))
+    got(bfull.at[c, z, mine, :], BACK + OVER)
+    move(held(bfull, 0, False), BACK + GX, xdev)
+    for k in range(2, 4):
+        to_partner(k)
+    lax.fori_loop(0, pairs // 4, mix_pair, 0)
+    got(bfull.at[c, z, other, :], BACK + GX)
+    gather_start(bfull, BACK, True)
+    lax.fori_loop(pairs // 4, pairs, mix_pair, 0)
     out_mixed = local(mixed, mixed_hbm, 6)
-
-    total = bcand[c, z].astype(F32)
-    for d in range(1, NZ):
-        got(brz.at[d], BZ_ + d)
-        total += brz[d].astype(F32)
-    bs[...] = total.astype(BF16)
-    send(bs.at[other, :], brx, BX, xdev)
-    got(brx, BX)
-    bchunk[...] = (bs[mine, :].astype(F32) + brx[...].astype(F32)).astype(BF16)
-    send(bchunk, bry, BY, ydev(2 - c))
-    got(bry, BY)
-    bfull[c, z, mine, :] = bry[...]
-    send(bry, bfull.at[c, z, mine, :], HX, xdev)
-    got(bfull.at[c, z, other, :], HX)
-    for d in range(1, NZ):
-        send(bfull.at[c, z], bfull.at[c, z], HZ_ + d, zdev(d))
-
-    for k in range(4):
+    gather_in(bfull, BACK, True, 2, (1, 2))
+    gather_in(bfull, BACK, True, -2, (-1,))
+
+    def total_k(k):
         got(precv.at[k], PIN_ + k)
         cols = slice(k * 1024, (k + 1) * 1024)
         igrad[:, cols] = (part[:, cols] + precv[k].astype(F32)).astype(BF16)
-    out_igrad = local(igrad, igrad_hbm, 7)
-
-    for d in range(1, NZ):
-        got(bfull.at[c, zat(-d)], HZ_ + d)
-    send(bfull.at[c], bfull.at[c], HCORE, sib)
-    got(bfull.at[1 - c], HCORE)
+
+    total_k(0)
+    total_k(1)
+    for d in (1, -1, 3, -3, 4):
+        gather_in(bfull, BACK, True, d)
+    gather_end(bfull, BACK)
     for k in range(2):
         m0, m1 = picked(0, k), picked(1, k)
         for zc in range(NZ):
@@ -377,6 +460,9 @@
                 )
                 dst[k, :, at : at + 128] = value.astype(BF16)
     out_a = local(agrad, agrad_hbm, 8)
+    total_k(2)
+    total_k(3)
+    out_igrad = local(igrad, igrad_hbm, 7)
     out_b = local(bgrad, bgrad_hbm, 9)
     for copy in sent:
         copy.wait_send()
@@ -390,13 +476,11 @@
 ):
     rows = tokens.shape[0]
     heads = decay_rate.shape[0]
-    location = owner_slot[tenant_list[0]]
-    loc = jnp.broadcast_to(jnp.pad(location, (0, 6))[:, None], (8, 128))
     a_t = jnp.swapaxes(a_store, 1, 2)
     half = inner_x.shape[1]
     cols = w_bc.shape[1]
-    rate = jnp.broadcast_to(decay_rate[:, None], (heads, rows))
-    hbm = pl.BlockSpec(memory_space=pl.ANY)
+    hbm = pl.BlockSpec(memory_space=pltpu.HBM)
+    free = pl.BlockSpec(memory_space=pl.ANY)
     vmem = pl.BlockSpec(memory_space=pltpu.VMEM)
     smem = pl.BlockSpec(memory_space=pltpu.SMEM)
     mixed, igrad, agrad, bgrad = pl.pallas_call(
@@ -407,8 +491,8 @@
             jax.ShapeDtypeStruct(a_t.shape, BF16),
             jax.ShapeDtypeStruct(b_store.shape, BF16),
         ),
-        in_specs=[smem, hbm, hbm, vmem, vmem, hbm, hbm, hbm, hbm, vmem],
-        out_specs=(hbm, hbm, hbm, hbm),
+        in_specs=[smem, smem, smem, smem, vmem, hbm, hbm, hbm, hbm, hbm, hbm],
+        out_specs=(free, free, free, free),
         scratch_shapes=[
             pltpu.VMEM((NZ, 1024, cols), BF16),
             pltpu.VMEM(tokens.shape, BF16),
@@ -416,12 +500,13 @@
             pltpu.VMEM((rows, half), BF16),
             pltpu.VMEM(a_t.shape, BF16),
             pltpu.VMEM(b_store.shape, BF16),
+            pltpu.VMEM((8, 128), jnp.int32),
             pltpu.VMEM((2, 8, 128), jnp.int32),
             pltpu.VMEM((2, NZ, 64, 640), BF16),
             pltpu.VMEM((NZ, 64, 640), BF16),
             pltpu.VMEM((NZ, 32, 640), BF16),
-            pltpu.VMEM((NZ, 32, 640), BF16),
-            pltpu.VMEM((32, 640), BF16),
+            pltpu.VMEM((3, 32, 640), BF16),
+            pltpu.VMEM((4, 32, 640), BF16),
             pltpu.VMEM((32, 640), BF16),
             pltpu.VMEM((2, NZ, 64, 640), BF16),
             pltpu.VMEM((64, half), BF16),
@@ -445,9 +530,9 @@
             pltpu.VMEM((rows, half), BF16),
             pltpu.VMEM((2, NZ, 64, 640), BF16),
             pltpu.VMEM((NZ, 64, 640), BF16),
-            pltpu.VMEM((NZ, 64, 640), BF16),
+            pltpu.VMEM((3, 64, 640), BF16),
+            pltpu.VMEM((4, 64, 640), BF16),
             pltpu.VMEM((64, 640), BF16),
-            pltpu.VMEM((32, 640), BF16),
             pltpu.VMEM((32, 640), BF16),
             pltpu.VMEM((32, 640), BF16),
             pltpu.VMEM((2, NZ, 64, 640), BF16),
@@ -460,7 +545,10 @@
         compiler_params=pltpu.CompilerParams(
             collective_id=0, has_side_effects=True, vmem_limit_bytes=56 * 1024 * 1024
         ),
-    )(block_slot, tokens, inner_x, step_size.T, rate, grad_out, w_bc, a_t, b_store, loc)
+    )(
+        block_slot, tenant_list, owner_slot, decay_rate, step_size.T,
+        tokens, inner_x, grad_out, w_bc, a_t, b_store,
+    )
     return mixed, igrad, jnp.swapaxes(agrad, 1, 2), bgrad
 
 

time: 147 us -> 126 us (0.86)
  Pallas kernels: 136 us -> 120 us
  local copies, waits for them, and re-layouts: 7.75 us -> 5.09 us
    pallas_call x1, Pallas kernels: 136 us -> 120 us  [shards(): pl.pallas_call(body, out_shape=(jax.ShapeDtypeStruct((rows, half), BF16),...]
    broadcast_in_dim x2 -> x0, local copies, waits for them, and re-layouts: 2.01 us -> none  [the longest x1 1.34 us: shards(): rate = jnp.broadcast_to(decay_rate[:, None], (heads, rows))]
    unnamed x12 -> x10, local copies, waits for them, and re-layouts: 5.1 us -> 5.09 us
where the time goes in v2:
time: 126 us
  Pallas kernels  120 us (95%)
  local copies, waits for them, and re-layouts  5.09 us (4%)
  between operations  1.31 us (1%)
    pallas_call x1, Pallas kernels, shards(): pl.pallas_call(body, out_shape=(jax.ShapeDtypeStruct((rows, half), BF16),...  120 us
    unnamed x10, local copies, waits for them, and re-layouts  5.09 us

profile of v2, /device:TPU:1, one launch (start us, length us, event | category | flops | bytes accessed | tf_op | source)
XLA Modules:
  0.0 126.2 jit_solution(1726652101905330929)
XLA Ops:
  1.3 119.8 %shard_map.138 = (bf16[128,4096]{1,0:T(8,128)(2,1)}, bf16[128,4096]{1,0:T(8,128)(2,1)}, bf16[2,64,4096]{2,1,0:T(8,128)(2,1)}, bf16[2,64,1024]{2,1,0:T(8,128)(2,1)}) custom-call(s32[1]{0:T(128)S(6)} %copy.19.slot_ref, s32[1,2]{1,0:T(1,128)} %list_ref.1, s32[256]{0:T(256)} %owner_ref.1, f32[64]{0:T(128)} %rate_ref.1, f32[64,128]{1,0:T(8,128)} %bitcast.5, ...), custom_call_target="tpu_custom_call" | custom-call | tf_op jit(solution)/shard_map/pallas_call | solution.py:486
  121.1 0.0 copy-start.1
  121.1 0.0 copy-start
  121.1 2.4 %copy.20 = bf16[128,4096]{1,0:T(8,128)(2,1)} copy(bf16[128,4096]{1,0:T(8,128)(2,1)} %get-tuple-element.16) | data formatting | bytes 2097152
  123.5 0.0 copy-done.1
  123.5 0.0 copy-start.2
  123.5 1.0 copy.21
  124.5 0.0 copy-done
  124.5 1.0 copy.22
  125.5 0.0 copy-done.2
  125.5 0.7 copy.23
Async XLA Ops:
  121.1 2.5 %copy-start.1 = (bf16[128,4096]{1,0:T(8,128)(2,1)S(1)}, bf16[128,4096]{1,0:T(8,128)(2,1)}, u32[]{:S(2)}) copy-start(bf16[128,4096]{1,0:T(8,128)(2,1)} %get-tuple-element.17) | copy-start | bytes 3145732
  121.1 3.4 %copy-start = (bf16[2,64,4096]{2,1,0:T(8,128)(2,1)S(1)}, bf16[2,64,4096]{2,1,0:T(8,128)(2,1)}, u32[]{:S(2)}) copy-start(bf16[2,64,4096]{2,1,0:T(8,128)(2,1)} %get-tuple-element.10) | copy-start | bytes 3145732
  123.5 1.9 %copy-start.2 = (bf16[2,64,1024]{2,1,0:T(8,128)(2,1)S(1)}, bf16[2,64,1024]{2,1,0:T(8,128)(2,1)}, u32[]{:S(2)}) copy-start(bf16[2,64,1024]{2,1,0:T(8,128)(2,1)} %get-tuple-element.19) | copy-start | bytes 786436

commit v3 on v2

--- a/solution.py
+++ b/solution.py
@@ -185,21 +185,29 @@
     mine = pl.ds(pl.multiple_of(32 * l, 32), 32)
     other = pl.ds(pl.multiple_of(32 * (1 - l), 32), 32)
 
+    turn = 1 - 2 * c
+
+    def zturn(d):
+        return zat(turn * d)
+
+    def zway(d):
+        return zdev(turn * d)
+
     def reduce_start(own, one, two, at):
-        send(own(3), one.at[0], at + Z1, zdev(1))
-        send(own(4), one.at[1], at + Z1 + 1, zdev(2))
-        send(own(-3), one.at[2], at + Z1 + 2, zdev(-1))
-        send(own(1), two.at[0], at + Z2, zdev(1))
-        send(own(-1), two.at[1], at + Z2 + 1, zdev(-1))
+        send(own(3), one.at[0], at + Z1, zway(1))
+        send(own(4), one.at[1], at + Z1 + 1, zway(2))
+        send(own(-3), one.at[2], at + Z1 + 2, zway(-1))
+        send(own(1), two.at[0], at + Z2, zway(1))
+        send(own(-1), two.at[1], at + Z2 + 1, zway(-1))
 
     def reduce_relay(own, one, two, at):
         for i in range(3):
             got(one.at[i], at + Z1 + i)
         up = one[0].astype(F32) + one[1].astype(F32) + own(2)[...].astype(F32)
         one[0] = up.astype(BF16)
-        send(one.at[0], two.at[2], at + Z2 + 2, zdev(2))
+        send(one.at[0], two.at[2], at + Z2 + 2, zway(2))
         one[2] = (one[2].astype(F32) + own(-2)[...].astype(F32)).astype(BF16)
-        send(one.at[2], two.at[3], at + Z2 + 3, zdev(-2))
+        send(one.at[2], two.at[3], at + Z2 + 3, zway(-2))
 
     def reduce_end(own, two, at):
         total = own(0)[...].astype(F32)
@@ -209,29 +217,29 @@
         return total
 
     def held(buf, d, wide):
-        return buf.at[c, zat(-d)] if wide else buf.at[c, zat(-d), mine, :]
+        return buf.at[c, zturn(-d)] if wide else buf.at[c, zturn(-d), mine, :]
 
     def gather_start(buf, at, wide):
         own = held(buf, 0, wide)
         for d in (2, -2, 1, -1):
-            move(own, at + GZ + d % 8, zdev(d))
+            move(own, at + GZ + d % 8, zway(d))
         move(own, at + (GC if wide else GX), sib if wide else xdev)
 
     def gather_in(buf, at, wide, d, hops=()):
         here = held(buf, d, wide)
         got(here, at + GZ + d % 8)
         for hop in hops:
-            move(here, at + GZ + (d + hop) % 8, zdev(hop))
+            move(here, at + GZ + (d + hop) % 8, zway(hop))
         move(here, at + (GC if wide else GX) + d % 8, sib if wide else xdev)
 
     def gather_core(buf, at, offs):
         for d in offs:
-            got(buf.at[c, zat(-d), other, :], at + GX + d % 8)
-            send(buf.at[c, zat(-d)], buf.at[c, zat(-d)], at + GC + d % 8, sib)
-
-    def gather_end(buf, at):
-        for d in range(NZ):
-            got(buf.at[1 - c, zat(-d)], at + GC + d)
+            got(buf.at[c, zturn(-d), other, :], at + GX + d % 8)
+            send(buf.at[c, zturn(-d)], buf.at[c, zturn(-d)], at + GC + d % 8, sib)
+
+    def gather_end(buf, at, offs):
+        for d in offs:
+            got(buf.at[1 - c, zturn(d)], at + GC + d % 8)
 
 
     def zstep(s, side):
@@ -285,7 +293,7 @@
     quarter = pairs // 4
 
     def own_rows(k):
-        return rx.at[zat(k)]
+        return rx.at[zturn(k)]
 
     for h in range(2):
         got(piece(0, 1, p, h), X_ + h)
@@ -335,7 +343,7 @@
     forward(3)
     gather_core(full, FETCH, (0, 2, -2, 1, -1, 3, -3, 4))
     ystep(4)
-    gather_end(full, FETCH)
+    gather_end(full, FETCH, range(NZ))
     slot = slot_ref[0]
     half = pl.multiple_of(t * 4096, 4096)
     low_part = jnp.zeros((64, rows), F32)
@@ -400,7 +408,7 @@
         return carry
 
     def own_sum(k):
-        return bcand.at[c, zat(k)]
+        return bcand.at[c, zturn(k)]
 
     got(brcore, BACK + CORE)
     for zc in range(NZ):
@@ -446,19 +454,29 @@
 
     total_k(0)
     total_k(1)
-    for d in (1, -1, 3, -3, 4):
+    masks = [[picked(j, k) for j in range(2)] for k in range(2)]
+
+    def place(offs):
+        for d in offs:
+            at = zat(d)
+            for k in range(2):
+                for i in range(5):
+                    dst, first = (agrad, at * 512 + i * 128) if i < 4 else (bgrad, at * 128)
+                    lane = slice(i * 128, (i + 1) * 128)
+                    value = (
+                        bfull[0, at, :, lane].astype(F32) * masks[k][0]
+                        + bfull[1, at, :, lane].astype(F32) * masks[k][1]
+                    )
+                    dst[k, :, pl.ds(pl.multiple_of(first, 128), 128)] = value.astype(BF16)
+
+    for d in (1, -1):
         gather_in(bfull, BACK, True, d)
-    gather_end(bfull, BACK)
-    for k in range(2):
-        m0, m1 = picked(0, k), picked(1, k)
-        for zc in range(NZ):
-            for i in range(5):
-                dst, at = (agrad, zc * 512 + i * 128) if i < 4 else (bgrad, zc * 128)
-                lane = slice(i * 128, (i + 1) * 128)
-                value = (
-                    bfull[0, zc, :, lane].astype(F32) * m0 + bfull[1, zc, :, lane].astype(F32) * m1
-                )
-                dst[k, :, at : at + 128] = value.astype(BF16)
+    gather_end(bfull, BACK, (0, 1, -1, 2, -2))
+    place((0, 1, -1, 2, -2))
+    for d in (3, -3, 4):
+        gather_in(bfull, BACK, True, d)
+    gather_end(bfull, BACK, (3, -3, 4))
+    place((3, -3, 4))
     out_a = local(agrad, agrad_hbm, 8)
     total_k(2)
     total_k(3)

time: 126 us -> 124 us (0.984)
  Pallas kernels: 120 us -> 118 us
    pallas_call x1, Pallas kernels: 120 us -> 118 us  [shards(): pl.pallas_call(body, out_shape=(jax.ShapeDtypeStruct((rows, half), BF16),...]
where the time goes in v3:
time: 124 us
  Pallas kernels  118 us (95%)
  local copies, waits for them, and re-layouts  5.09 us (4%)
  between operations  1.31 us (1%)
    pallas_call x1, Pallas kernels, shards(): pl.pallas_call(body, out_shape=(jax.ShapeDtypeStruct((rows, half), BF16),...  118 us
    unnamed x10, local copies, waits for them, and re-layouts  5.09 us

profile of v3, /device:TPU:1, one launch (start us, length us, event | category | flops | bytes accessed | tf_op | source)
XLA Modules:
  0.0 124.0 jit_solution(5490182732532498992)
XLA Ops:
  1.3 117.6 %shard_map.138 = (bf16[128,4096]{1,0:T(8,128)(2,1)}, bf16[128,4096]{1,0:T(8,128)(2,1)}, bf16[2,64,4096]{2,1,0:T(8,128)(2,1)}, bf16[2,64,1024]{2,1,0:T(8,128)(2,1)}) custom-call(s32[1]{0:T(128)S(6)} %copy.19.slot_ref, s32[1,2]{1,0:T(1,128)} %list_ref.1, s32[256]{0:T(256)} %owner_ref.1, f32[64]{0:T(128)} %rate_ref.1, f32[64,128]{1,0:T(8,128)} %bitcast.5, ...), custom_call_target="tpu_custom_call" | custom-call | tf_op jit(solution)/shard_map/pallas_call | solution.py:504
  118.9 0.0 copy-start.1
  118.9 0.0 copy-start
  119.0 2.4 %copy.20 = bf16[128,4096]{1,0:T(8,128)(2,1)} copy(bf16[128,4096]{1,0:T(8,128)(2,1)} %get-tuple-element.16) | data formatting | bytes 2097152
  121.4 0.0 copy-done.1
  121.4 0.0 copy-start.2
  121.4 1.0 copy.21
  122.4 0.0 copy-done
  122.4 1.0 copy.22
  123.3 0.0 copy-done.2
  123.3 0.7 copy.23
Async XLA Ops:
  118.9 2.5 %copy-start.1 = (bf16[128,4096]{1,0:T(8,128)(2,1)S(1)}, bf16[128,4096]{1,0:T(8,128)(2,1)}, u32[]{:S(2)}) copy-start(bf16[128,4096]{1,0:T(8,128)(2,1)} %get-tuple-element.17) | copy-start | bytes 3145732
  118.9 3.4 %copy-start = (bf16[2,64,4096]{2,1,0:T(8,128)(2,1)S(1)}, bf16[2,64,4096]{2,1,0:T(8,128)(2,1)}, u32[]{:S(2)}) copy-start(bf16[2,64,4096]{2,1,0:T(8,128)(2,1)} %get-tuple-element.10) | copy-start | bytes 3145732
  121.4 1.9 %copy-start.2 = (bf16[2,64,1024]{2,1,0:T(8,128)(2,1)S(1)}, bf16[2,64,1024]{2,1,0:T(8,128)(2,1)}, u32[]{:S(2)}) copy-start(bf16[2,64,1024]{2,1,0:T(8,128)(2,1)} %get-tuple-element.19) | copy-start | bytes 786436

commit v4 on v3

--- a/solution.py
+++ b/solution.py
@@ -359,18 +359,17 @@
     low_t[...] = (low_s[...] + low_r[...]).astype(BF16)
     proj[...] = (acc[...] + dot(low_t[...], sel_b[...], TN)).astype(BF16)
 
-    scores = []
     for gi in range(2):
         b_in = proj[:, gi * 512 : gi * 512 + 256]
         c_out = proj[:, gi * 512 + 256 : gi * 512 + 512]
-        scores.append(dot(c_out, b_in, NT))
         sg = score_grad[gi].astype(BF16)
         gproj[:, gi * 512 : gi * 512 + 256] = dot(sg, c_out, TN).astype(BF16)
         gproj[:, gi * 512 + 256 : gi * 512 + 512] = dot(sg, b_in).astype(BF16)
     q_s[...] = dot(sel_b[...], gproj[...], NT)
     send(q_s, q_r, Q, tdev)
     for gi in range(2):
-        score_grad[gi] = scores[gi]
+        c_out = proj[:, gi * 512 + 256 : gi * 512 + 512]
+        score_grad[gi] = dot(c_out, proj[:, gi * 512 : gi * 512 + 256], NT)
 
     def back(at, n):
         return dot(gproj[...], w[at, pl.ds(pl.multiple_of(n * 256, 256), 256), :], NT)
@@ -415,6 +414,7 @@
         bcand[c, zc] = (bcand[c, zc].astype(F32) + brcore[zc].astype(F32)).astype(BF16)
     reduce_start(own_sum, br1, br2, BACK)
     partner(2)
+    to_partner(2)
     partner(3)
     lax.fori_loop(0, 5, own_n, 0)
     reduce_relay(own_sum, br1, br2, BACK)
@@ -437,8 +437,7 @@
     send(bchunk, bfull.at[c, z, mine, :], BACK + OVER, ydev(2 - c))
     got(bfull.at[c, z, mine, :], BACK + OVER)
     move(held(bfull, 0, False), BACK + GX, xdev)
-    for k in range(2, 4):
-        to_partner(k)
+    to_partner(3)
     lax.fori_loop(0, pairs // 4, mix_pair, 0)
     got(bfull.at[c, z, other, :], BACK + GX)
     gather_start(bfull, BACK, True)
@@ -473,12 +472,12 @@
         gather_in(bfull, BACK, True, d)
     gather_end(bfull, BACK, (0, 1, -1, 2, -2))
     place((0, 1, -1, 2, -2))
+    total_k(2)
     for d in (3, -3, 4):
         gather_in(bfull, BACK, True, d)
     gather_end(bfull, BACK, (3, -3, 4))
     place((3, -3, 4))
     out_a = local(agrad, agrad_hbm, 8)
-    total_k(2)
     total_k(3)
     out_igrad = local(igrad, igrad_hbm, 7)
     out_b = local(bgrad, bgrad_hbm, 9)

time: 124 us -> 124 us (level)
  no operation moved by 1% of the time
where the time goes in v4:
time: 124 us
  Pallas kernels  117 us (94%)
  local copies, waits for them, and re-layouts  5.09 us (4%)
  between operations  1.31 us (1%)
    pallas_call x1, Pallas kernels, shards(): pl.pallas_call(body, out_shape=(jax.ShapeDtypeStruct((rows, half), BF16),...  117 us
    unnamed x10, local copies, waits for them, and re-layouts  5.09 us

profile of v4, /device:TPU:1, one launch (start us, length us, event | category | flops | bytes accessed | tf_op | source)
XLA Modules:
  0.0 123.5 jit_solution(16158722337415444396)
XLA Ops:
  1.3 117.1 %shard_map.138 = (bf16[128,4096]{1,0:T(8,128)(2,1)}, bf16[128,4096]{1,0:T(8,128)(2,1)}, bf16[2,64,4096]{2,1,0:T(8,128)(2,1)}, bf16[2,64,1024]{2,1,0:T(8,128)(2,1)}) custom-call(s32[1]{0:T(128)S(6)} %copy.19.slot_ref, s32[1,2]{1,0:T(1,128)} %list_ref.1, s32[256]{0:T(256)} %owner_ref.1, f32[64]{0:T(128)} %rate_ref.1, f32[64,128]{1,0:T(8,128)} %bitcast.5, ...), custom_call_target="tpu_custom_call" | custom-call | tf_op jit(solution)/shard_map/pallas_call | solution.py:503
  118.4 0.0 copy-start.1
  118.4 0.0 copy-start
  118.4 2.4 %copy.20 = bf16[128,4096]{1,0:T(8,128)(2,1)} copy(bf16[128,4096]{1,0:T(8,128)(2,1)} %get-tuple-element.16) | data formatting | bytes 2097152
  120.9 0.0 copy-done.1
  120.9 0.0 copy-start.2
  120.9 1.0 copy.21
  121.9 0.0 copy-done
  121.9 1.0 copy.22
  122.8 0.0 copy-done.2
  122.8 0.7 copy.23
Async XLA Ops:
  118.4 2.5 %copy-start.1 = (bf16[128,4096]{1,0:T(8,128)(2,1)S(1)}, bf16[128,4096]{1,0:T(8,128)(2,1)}, u32[]{:S(2)}) copy-start(bf16[128,4096]{1,0:T(8,128)(2,1)} %get-tuple-element.17) | copy-start | bytes 3145732
  118.4 3.4 %copy-start = (bf16[2,64,4096]{2,1,0:T(8,128)(2,1)S(1)}, bf16[2,64,4096]{2,1,0:T(8,128)(2,1)}, u32[]{:S(2)}) copy-start(bf16[2,64,4096]{2,1,0:T(8,128)(2,1)} %get-tuple-element.10) | copy-start | bytes 3145732
  120.9 1.9 %copy-start.2 = (bf16[2,64,1024]{2,1,0:T(8,128)(2,1)S(1)}, bf16[2,64,1024]{2,1,0:T(8,128)(2,1)}, u32[]{:S(2)}) copy-start(bf16[2,64,1024]{2,1,0:T(8,128)(2,1)} %get-tuple-element.19) | copy-start | bytes 786436

commit v5 on v4

--- a/solution.py
+++ b/solution.py
@@ -416,6 +416,7 @@
     partner(2)
     to_partner(2)
     partner(3)
+    to_partner(3)
     lax.fori_loop(0, 5, own_n, 0)
     reduce_relay(own_sum, br1, br2, BACK)
     lax.fori_loop(5, 16, own_n, 0)
@@ -435,24 +436,20 @@
     got(brx, BACK + ACROSS)
     bchunk[...] = (bs[mine, :].astype(F32) + brx[...].astype(F32)).astype(BF16)
     send(bchunk, bfull.at[c, z, mine, :], BACK + OVER, ydev(2 - c))
+    lax.fori_loop(0, pairs // 4, mix_pair, 0)
     got(bfull.at[c, z, mine, :], BACK + OVER)
-    move(held(bfull, 0, False), BACK + GX, xdev)
-    to_partner(3)
-    lax.fori_loop(0, pairs // 4, mix_pair, 0)
-    got(bfull.at[c, z, other, :], BACK + GX)
-    gather_start(bfull, BACK, True)
-    lax.fori_loop(pairs // 4, pairs, mix_pair, 0)
+    gather_start(bfull, BACK, False)
+    lax.fori_loop(pairs // 4, pairs // 2, mix_pair, 0)
+    gather_in(bfull, BACK, False, 2, (1, 2))
+    gather_in(bfull, BACK, False, -2, (-1,))
+    lax.fori_loop(pairs // 2, pairs, mix_pair, 0)
     out_mixed = local(mixed, mixed_hbm, 6)
-    gather_in(bfull, BACK, True, 2, (1, 2))
-    gather_in(bfull, BACK, True, -2, (-1,))
 
     def total_k(k):
         got(precv.at[k], PIN_ + k)
         cols = slice(k * 1024, (k + 1) * 1024)
         igrad[:, cols] = (part[:, cols] + precv[k].astype(F32)).astype(BF16)
 
-    total_k(0)
-    total_k(1)
     masks = [[picked(j, k) for j in range(2)] for k in range(2)]
 
     def place(offs):
@@ -469,12 +466,16 @@
                     dst[k, :, pl.ds(pl.multiple_of(first, 128), 128)] = value.astype(BF16)
 
     for d in (1, -1):
-        gather_in(bfull, BACK, True, d)
+        gather_in(bfull, BACK, False, d)
+    total_k(0)
+    total_k(1)
+    gather_core(bfull, BACK, (0, 2, -2, 1, -1))
+    for d in (3, -3, 4):
+        gather_in(bfull, BACK, False, d)
+    total_k(2)
+    gather_core(bfull, BACK, (3, -3, 4))
     gather_end(bfull, BACK, (0, 1, -1, 2, -2))
     place((0, 1, -1, 2, -2))
-    total_k(2)
-    for d in (3, -3, 4):
-        gather_in(bfull, BACK, True, d)
     gather_end(bfull, BACK, (3, -3, 4))
     place((3, -3, 4))
     out_a = local(agrad, agrad_hbm, 8)

time: 124 us -> 129 us (1.040)
  Pallas kernels: 117 us -> 122 us
    pallas_call x1, Pallas kernels: 117 us -> 122 us  [shards(): pl.pallas_call(body, out_shape=(jax.ShapeDtypeStruct((rows, half), BF16),...]
where the time goes in v5:
time: 129 us
  Pallas kernels  122 us (95%)
  local copies, waits for them, and re-layouts  5.09 us (4%)
  between operations  1.31 us (1%)
    pallas_call x1, Pallas kernels, shards(): pl.pallas_call(body, out_shape=(jax.ShapeDtypeStruct((rows, half), BF16),...  122 us
    unnamed x10, local copies, waits for them, and re-layouts  5.09 us

profile of v5, /device:TPU:1, one launch (start us, length us, event | category | flops | bytes accessed | tf_op | source)
XLA Modules:
  0.0 128.6 jit_solution(4364155346035836852)
XLA Ops:
  1.3 122.2 %shard_map.138 = (bf16[128,4096]{1,0:T(8,128)(2,1)}, bf16[128,4096]{1,0:T(8,128)(2,1)}, bf16[2,64,4096]{2,1,0:T(8,128)(2,1)}, bf16[2,64,1024]{2,1,0:T(8,128)(2,1)}) custom-call(s32[1]{0:T(128)S(6)} %copy.19.slot_ref, s32[1,2]{1,0:T(1,128)} %list_ref.1, s32[256]{0:T(256)} %owner_ref.1, f32[64]{0:T(128)} %rate_ref.1, f32[64,128]{1,0:T(8,128)} %bitcast.5, ...), custom_call_target="tpu_custom_call" | custom-call | tf_op jit(solution)/shard_map/pallas_call | solution.py:504
  123.5 0.0 copy-start.1
  123.5 0.0 copy-start
  123.5 2.4 %copy.20 = bf16[128,4096]{1,0:T(8,128)(2,1)} copy(bf16[128,4096]{1,0:T(8,128)(2,1)} %get-tuple-element.16) | data formatting | bytes 2097152
  126.0 0.0 copy-done.1
  126.0 0.0 copy-start.2
  126.0 1.0 copy.21
  127.0 0.0 copy-done
  127.0 1.0 copy.22
  127.9 0.0 copy-done.2
  127.9 0.7 copy.23
Async XLA Ops:
  123.5 2.5 %copy-start.1 = (bf16[128,4096]{1,0:T(8,128)(2,1)S(1)}, bf16[128,4096]{1,0:T(8,128)(2,1)}, u32[]{:S(2)}) copy-start(bf16[128,4096]{1,0:T(8,128)(2,1)} %get-tuple-element.17) | copy-start | bytes 3145732
  123.5 3.4 %copy-start = (bf16[2,64,4096]{2,1,0:T(8,128)(2,1)S(1)}, bf16[2,64,4096]{2,1,0:T(8,128)(2,1)}, u32[]{:S(2)}) copy-start(bf16[2,64,4096]{2,1,0:T(8,128)(2,1)} %get-tuple-element.10) | copy-start | bytes 3145732
  126.0 1.9 %copy-start.2 = (bf16[2,64,1024]{2,1,0:T(8,128)(2,1)S(1)}, bf16[2,64,1024]{2,1,0:T(8,128)(2,1)}, u32[]{:S(2)}) copy-start(bf16[2,64,1024]{2,1,0:T(8,128)(2,1)} %get-tuple-element.19) | copy-start | bytes 786436
